TPU v7x, 32 devices: a whole 2x2x4 slice. The times are simulated.
32 devices in a mesh: win: 8 (over z, y), space: 4 (over x, core).
Axes of the slice: x: 2, y: 2, z: 4, core: 2. Of those that a mesh axis runs over, the one named last changes fastest.
Arguments:
- increment: float32 [8, 64, 256, 256], P('win', 'space'), may hold values from -6 to 6
- multiplier: float32 [8, 64, 256, 256], P('win', 'space'), may hold values from -6 to 6
- obs_dual: float32 [8, 4096], P('win', 'space'), may hold values from -6 to 6
- obs_sites: int32 [8, 3, 4096], P('win'), may hold values from 0 to 255, as said below
- obs_variance: float32 [8, 4096], P('win', 'space'), may hold values from 0.5 to 2
- trajectory: bfloat16 [8, 64, 256, 256], P('win', None, 'space'), may hold values from -6 to 6
- diffusion: float32 [64], replicated, may hold values from 0.05 to 0.2
- drift_rows: float32 [64], replicated, may hold values from -0.25 to 0.25
- drift_cols: float32 [64], replicated, may hold values from -0.25 to 0.25
- spread: float32 [64], replicated, may hold values from 0.5 to 2
- row_factor: float32 [256, 256], replicated, may hold values from -0.375 to 0.375
- col_factor: float32 [256, 256], replicated, may hold values from -0.375 to 0.375
- layer_in: bfloat16 [1024, 64], replicated, may hold values from -0.75 to 0.75
- bias_in: float32 [1024], replicated, may hold values from -4 to 4
- layer_out: bfloat16 [64, 1024], replicated, may hold values from -0.1875 to 0.1875
Outputs:
- state_out: float32 [8, 64, 256, 256], P('win', 'space')
- obs_out: float32 [8, 4096], P('win', 'space')
- mult_out: float32 [8, 64, 256, 256], P('win', 'space')
Inputs may be any that keep to these rules, and one draw needn't show every extreme that they name: `obs_sites`: row 0 holds a level below 64, row 1 a first index below 256, row 2 a second index below 256; positions may repeat.
All inputs are finite; a program needn't handle non-finite values.
Results may differ from a plain program's by a relative error of at most 0.0011.
Values sent between devices are 32-bit elements; how exact they have to be, the bound alone decides.
No kernel may reach another device: no remote copies, remote signals or barrier semaphores. Data moves between devices by JAX's collectives and lax.ppermute only.
A program may use at most 128 MiB of HBM per device.

v0:
```python
import jax
import jax.numpy as jnp
from jax import lax
from jax.sharding import PartitionSpec as P

STEPS = 4


exact_mode = lax.Precision.HIGHEST


def from_behind(value, axis, steps):
    count = lax.axis_size(axis)
    first, last = (max(0, -steps), min(count, count - steps))
    return lax.ppermute(value, axis, [(source, source + steps) for source in range(first, last)])


def stencil_step(padded, diffusion, drift_rows, drift_cols, direction):
    centre = padded[:, 1:-1, :]
    row_up = padded[:, 2:, :]
    row_down = padded[:, :-2, :]
    widened = jnp.pad(centre, ((0, 0), (0, 0), (1, 1)))
    col_up = widened[:, :, 2:]
    col_down = widened[:, :, :-2]
    mixing = row_up + row_down + col_up + col_down - 4.0 * centre
    carried = drift_rows * (row_up - row_down) + drift_cols * (col_up - col_down)
    return centre + diffusion * mixing - direction * carried


def network_both(forward_in, backward_in, trajectory, layer_in, bias_in, layer_out):
    levels, row_count, columns = forward_in.shape
    block_rows = min(row_count, max(1, 1024 // columns))

    def select(source, first_row):
        piece = lax.dynamic_slice_in_dim(source, first_row, block_rows, 1)
        return piece.reshape(levels, block_rows * columns)

    def visit(block_index, totals):
        first_row = (block_index * block_rows).astype(jnp.int32)
        path = select(trajectory, first_row)
        activation = jnp.dot(layer_in, path, preferred_element_type=jnp.float32) + bias_in[:, None]
        gating = jax.nn.sigmoid(activation)
        slopes = gating * (1.0 + activation * (1.0 - gating))
        tangent_in = select(forward_in, first_row)
        hidden = (
            slopes
            * jnp.dot(layer_in, tangent_in.astype(jnp.bfloat16), preferred_element_type=jnp.float32)
        ).astype(jnp.bfloat16)
        tangent_out = tangent_in + jnp.dot(layer_out, hidden, preferred_element_type=jnp.float32)
        adjoint_in = select(backward_in, first_row)
        back_hidden = (
            slopes
            * jnp.dot(
                layer_out.T, adjoint_in.astype(jnp.bfloat16), preferred_element_type=jnp.float32
            )
        ).astype(jnp.bfloat16)
        adjoint_out = adjoint_in + jnp.dot(
            layer_in.T, back_hidden, preferred_element_type=jnp.float32
        )
        shape = (levels, block_rows, columns)
        return (
            lax.dynamic_update_slice_in_dim(totals[0], tangent_out.reshape(shape), first_row, 1),
            lax.dynamic_update_slice_in_dim(totals[1], adjoint_out.reshape(shape), first_row, 1),
        )

    empty = jnp.zeros(forward_in.shape, jnp.float32)
    return lax.fori_loop(0, row_count // block_rows, visit, (empty, empty))


def correlate(fields, spread, row_factor, col_factor):
    inner = jnp.einsum("xa,lxy->lay", row_factor, fields, precision=exact_mode)
    inner = jnp.einsum("lay,yb->lab", inner, col_factor, precision=exact_mode)
    outer = jnp.einsum("xa,lab->lxb", row_factor, inner, precision=exact_mode)
    outer = jnp.einsum("lxb,yb->lxy", outer, col_factor, precision=exact_mode)
    return (spread * spread)[:, None, None] * outer


def slab_steps(fields, coefs, direction):
    for repeat in range(STEPS):
        padded = jnp.pad(fields, ((0, 0), (1, 1), (0, 0)))
        fields = stencil_step(padded, coefs[0], coefs[1], coefs[2], direction)
    return fields


def body(
    increment,
    multiplier,
    obs_dual,
    obs_sites,
    obs_variance,
    trajectory,
    diffusion,
    drift_rows,
    drift_cols,
    spread,
    row_factor,
    col_factor,
    layer_in,
    bias_in,
    layer_out,
):
    level_count = increment.shape[1]
    grid_rows = increment.shape[2]
    grid_cols = increment.shape[3]
    space_index = lax.axis_index("space")
    level_first = space_index * level_count

    def local_coefs(values):
        return lax.dynamic_slice_in_dim(values, level_first, level_count)[:, None, None]

    slab_coefs = (local_coefs(diffusion), local_coefs(drift_rows), local_coefs(drift_cols))
    own_state = increment[0]
    own_mult = multiplier[0]
    previous = from_behind(own_state, "win", 1)
    outgoing = slab_steps(previous, slab_coefs, 1.0)
    strip_state, strip_mult = (
        lax.all_to_all(outgoing, "space", split_axis=1, concat_axis=0, tiled=True),
        lax.all_to_all(own_mult, "space", split_axis=1, concat_axis=0, tiled=True),
    )
    forward, backward = network_both(
        strip_state, strip_mult, trajectory[0], layer_in, bias_in, layer_out
    )
    slab_forward, slab_backward = (
        lax.all_to_all(forward, "space", split_axis=0, concat_axis=1, tiled=True),
        lax.all_to_all(backward, "space", split_axis=0, concat_axis=1, tiled=True),
    )
    slab_backward = slab_steps(slab_backward, slab_coefs, -1.0)
    later = from_behind(slab_backward, "win", -1)
    local_spread = lax.dynamic_slice_in_dim(spread, level_first, level_count)
    correlated = correlate(own_mult, local_spread, row_factor, col_factor)
    state_out = correlated + own_state - slab_forward
    duals = lax.all_gather(obs_dual[0], "space", axis=0, tiled=True)
    positions = obs_sites[0]
    local_level = positions[0] - level_first
    inside = (local_level >= 0) & (local_level < level_count)
    row_total = level_count * grid_rows
    row_index = jnp.where(inside, local_level * grid_rows + positions[1], row_total)
    block_size = obs_dual.shape[1]
    block_count = positions.shape[1] // block_size
    index_blocks = row_index.reshape(block_count, block_size)
    column_blocks = positions[2].reshape(block_count, block_size)
    dual_blocks = duals.reshape(block_count, block_size)
    flat_state = own_state.reshape(row_total, grid_cols)
    column_ids = lax.iota(jnp.int32, grid_cols)[None, :]

    def pick_block(block_items):
        block_rows_index, block_columns = block_items
        picked = jnp.take(flat_state, block_rows_index, axis=0, mode="fill", fill_value=0.0)
        chosen = column_ids == block_columns[:, None]
        return jnp.sum(jnp.where(chosen, picked, 0.0), axis=1)

    seen = lax.map(pick_block, (index_blocks, column_blocks)).reshape(-1)
    partial_value = lax.psum_scatter(seen, "space", scatter_dimension=0, tiled=True)
    obs_out = obs_variance[0] * obs_dual[0] + partial_value

    def add_block(block_number, total):
        block_rows_index = index_blocks[block_number]
        chosen = column_ids == column_blocks[block_number][:, None]
        spread_rows = jnp.where(chosen, dual_blocks[block_number][:, None], 0.0)
        return total.at[block_rows_index].add(spread_rows, mode="drop")

    placed_rows = lax.fori_loop(
        0, block_count, add_block, jnp.zeros((row_total, grid_cols), jnp.float32)
    )
    placed = placed_rows.reshape(level_count, grid_rows, grid_cols)
    mult_out = own_mult - later + placed
    return (state_out[None], obs_out[None], mult_out[None])


def solution(mesh):
    placed = (
        P("win", "space", None, None),
        P("win", "space", None, None),
        P("win", "space"),
        P("win", None, None),
        P("win", "space"),
        P("win", None, "space", None),
        P(),
        P(),
        P(),
        P(),
        P(),
        P(),
        P(),
        P(),
        P(),
    )
    return jax.shard_map(
        body,
        mesh=mesh,
        in_specs=placed,
        out_specs=(P("win", "space", None, None), P("win", "space"), P("win", "space", None, None)),
        check_vma=False,
    )
```

profile of v0, /device:TPU:0, one launch (start us, length us, event | category | flops | bytes accessed | tf_op | source)
XLA Modules:
  0.0 638.6 jit_solution(11368986352953169115)
XLA Ops:
  0.6 7.0 %collective-permute-start = (f32[16,256,256]{2,1,0:T(8,128)}, f32[16,256,256]{2,1,0:T(8,128)}, u32[]{:S(2)}, u32[]{:S(2)}) collective-permute-start(f32[16,256,256]{2,1,0:T(8,128)} %bitcast.178), channel_id=1, source_target_pairs={{0,4},{4,8},{8,12},{12,16},{16,20},{20,24},{24,28},{1,5},{5,9},{9,... | collective-permute-start | bytes 12582920 | tf_op jit(solution)/shard_map/ppermute | solution.py:15
  7.6 6.6 %copy.32 = f32[16,256,256]{2,0,1:T(8,128)} copy(f32[16,256,256]{2,1,0:T(8,128)} %bitcast.181) | data formatting | bytes 8388608 | tf_op jit(solution)/shard_map/squeeze | solution.py:113
  14.2 5.3 all-to-all-start.1
  19.8 76.0 %collective-permute-done = f32[16,256,256]{2,1,0:T(8,128)} collective-permute-done((f32[16,256,256]{2,1,0:T(8,128)}, f32[16,256,256]{2,1,0:T(8,128)}, u32[]{:S(2)}, u32[]{:S(2)}) %collective-permute-start) | collective-permute-done | bytes 4194336 | tf_op jit(solution)/shard_map/ppermute | solution.py:15
  95.8 10.9 %add_subtract_fusion.3 = f32[16,256,256]{2,1,0:T(8,128)S(1)} fusion(f32[16,256,256]{2,1,0:T(8,128)} %collective-permute-done, f32[16]{0:T(128)S(1)} %dynamic_slice.64, f32[16]{0:T(128)S(1)} %dynamic_slice.63, f32[16]{0:T(128)S(1)} %dynamic_slice.62), kind=kLoop, calls=%fused_computation.74 | loop fusion | flops 13631488 | bytes 8388800 | tf_op jit(solution)/shard_map/sub | solution.py:27
  106.7 3.8 add_subtract_fusion.2
  110.5 3.8 add_subtract_fusion.1
  114.4 3.8 add_subtract_fusion
  118.3 4.4 copy.30
  122.7 5.5 all-to-all-start
  128.2 6.6 %copy.33 = f32[4,16,64,256]{3,2,1,0:T(8,128)} copy(f32[4,16,64,256]{3,1,2,0:T(8,128)} %bitcast.16) | data formatting | bytes 8388608 | tf_op jit(solution)/shard_map/all_to_all | solution.py:118
  134.7 41.6 %all-to-all-done = f32[16,256,256]{2,0,1:T(8,128)} async-done(((f32[16,256,256]{2,0,1:T(8,128)}), f32[16,256,256]{2,0,1:T(8,128)}, u32[]{:S(2)}, u32[]{:S(2)}) %all-to-all-start) | async-done | bytes 4194336 | tf_op jit(solution)/shard_map/all_to_all | solution.py:117
  176.4 6.6 %copy.31 = f32[4,16,64,256]{3,2,1,0:T(8,128)} copy(f32[4,16,64,256]{3,1,2,0:T(8,128)} %bitcast.12) | data formatting | bytes 8388608 | tf_op jit(solution)/shard_map/all_to_all | solution.py:117
  188.0 241.9 %while.40 = (s32[]{:T(128)}, f32[64,64,256]{2,1,0:T(8,128)}, f32[64,64,256]{2,1,0:T(8,128)}, f32[64,64,256]{2,1,0:T(8,128)}, bf16[64,64,256]{2,1,0:T(8,128)(2,1)...) while((s32[]{:T(128)}, f32[64,64,256]{2,1,0:T(8,128)}, ...), condition=%wide.region_1.2_spmd, body=%wide.region_0.1_spmd.sunk | while | flops 683933696 | bytes 19140796 | solution.py:67
  189.1 3.6 fusion.70
  198.7 3.5 fusion.71
  204.2 3.6 fusion.70
  209.0 3.5 fusion.72
  219.3 3.6 fusion.70
  228.9 3.5 fusion.71
  234.4 3.6 fusion.70
  239.2 3.5 fusion.72
  249.6 3.6 fusion.70
  259.1 3.5 fusion.71
  264.7 3.6 fusion.70
  279.8 3.6 fusion.70
  289.3 3.5 fusion.71
  294.9 3.6 fusion.70
  310.0 3.6 fusion.70
  319.6 3.5 fusion.71
  325.1 3.6 fusion.70
  340.3 3.6 fusion.70
  349.8 3.5 fusion.71
  355.4 3.6 fusion.70
  370.5 3.6 fusion.70
  380.0 3.5 fusion.71
  385.6 3.6 fusion.70
  400.7 3.6 fusion.70
  410.3 3.5 fusion.71
  415.8 3.6 fusion.70
  429.9 5.0 all-to-all-start.3
  435.0 48.1 %all-to-all-done.3 = f32[64,64,256]{2,1,0:T(8,128)} async-done(((f32[64,64,256]{2,1,0:T(8,128)}), f32[64,64,256]{2,1,0:T(8,128)}, u32[]{:S(2)}, u32[]{:S(2)}) %all-to-all-start.3) | async-done | bytes 4194336 | tf_op jit(solution)/shard_map/all_to_all | solution.py:125
  483.1 5.0 all-to-all-start.2
  490.8 3.7 multiply_subtract_fusion.3
  494.6 3.7 multiply_subtract_fusion.2
  498.3 3.7 multiply_subtract_fusion.1
  502.0 5.4 multiply_subtract_fusion
  508.8 25.3 %while.41 = (s32[]{:T(128)}, f32[4,1024]{1,0:T(4,128)S(1)}, s32[4,1024]{1,0:T(4,128)S(1)}, s32[4,1024]{1,0:T(4,128)S(1)}, f32[4096,256]{1,0:T(8,128)}, /*index=5*/s32[]{:T(128)}, s32[]{:T(128)}) while((s32[]{:T(128)}, f32[4,1024]{1,0:T(4,128)S(1)}, s32[4,1024]{1,0:T(4,128)S(1)}, s32[4,1024]{1,0:T(4,128)S(1)}, ...), condition=%wide.region_4.5_spmd.clone, body=%wide.region_2.4_spmd.clone.sunk | while | flops 1057794 | bytes 3201113 | solution.py:152
  508.8 5.7 gather_fusion
  515.1 5.7 gather_fusion
  521.5 5.7 gather_fusion
  527.8 5.7 gather_fusion
  534.1 5.3 all-gather
  541.9 12.9 %all-reduce.16 = f32[4096]{0:T(1024)S(1)} all-reduce(f32[4096]{0:T(1024)S(1)} %bitcast.200), channel_id=3, replica_groups=mesh['win'=8,'space'=4] {'space'}, use_global_device_ids=true, to_apply=%region_5.6.clone | all-reduce | flops 4096 | bytes 32768
  555.4 8.8 %fusion.39 = f32[16,256,256]{2,1,0:T(8,128)S(1)} fusion(f32[256,256]{1,0:T(8,128)S(1)} %copy-done, f32[1,16,256,256]{3,2,1,0:T(8,128)} %param.22), kind=kOutput, calls=%fused_computation.80 | convolution fusion | flops 3221225472 | bytes 8650752 | tf_op jit(solution)/shard_map/xa,lxy->lay/dot_general | solution.py:71
  564.3 4.3 fusion.28
  568.6 5.0 fusion.37
  575.8 43.5 %while.42 = (s32[]{:T(128)}, f32[4096,256]{1,0:T(8,128)}, s32[4,1024]{1,0:T(4,128)S(1)}, s32[4,1024]{1,0:T(4,128)S(1)}, f32[4,1024]{1,0:T(4,128)S(1)}, /*index=5*/s32[]{:T(128)}, f32[]{:T(128)}) while((s32[]{:T(128)}, f32[4096,256]{1,0:T(8,128)}, s32[4,1024]{1,0:T(4,128)S(1)}, s32[4,1024]{1,0:T(4,128)S(1)}, ...), condition=%wide.region_8.9_spmd.clone, body=%wide.region_6.8_spmd.clone.sunk | while | flops 789506 | bytes 4227673 | solution.py:162
  576.1 10.8 %scatter_custom_fusion.6 = f32[4096,256]{1,0:T(8,128)} fusion(f32[4096,256]{1,0:T(8,128)} %get-tuple-element.564, s32[1024]{0:T(1024)S(1)} %bitcast.199, f32[]{:T(128)} %constant.115.clone.1..sunk, f32[1024]{0:T(1024)S(1)} %bitcast.196, s32[1024]{0:T(1024)S(1)} %bitcast.197), kind=kCustom, calls=%fused_computation.37.clone.1 | custom fusion | flops 786432 | bytes 4203008 | tf_op jit(solution)/shard_map/while/body/eval_jaxpr/scatter-add | solution.py:160
  586.9 10.8 %scatter_custom_fusion.6 = f32[4096,256]{1,0:T(8,128)} fusion(f32[4096,256]{1,0:T(8,128)} %get-tuple-element.564, s32[1024]{0:T(1024)S(1)} %bitcast.199, f32[]{:T(128)} %constant.115.clone.1..sunk, f32[1024]{0:T(1024)S(1)} %bitcast.196, s32[1024]{0:T(1024)S(1)} %bitcast.197), kind=kCustom, calls=%fused_computation.37.clone.1 | custom fusion | flops 786432 | bytes 4203008 | tf_op jit(solution)/shard_map/while/body/eval_jaxpr/scatter-add | solution.py:160
  597.7 10.8 %scatter_custom_fusion.6 = f32[4096,256]{1,0:T(8,128)} fusion(f32[4096,256]{1,0:T(8,128)} %get-tuple-element.564, s32[1024]{0:T(1024)S(1)} %bitcast.199, f32[]{:T(128)} %constant.115.clone.1..sunk, f32[1024]{0:T(1024)S(1)} %bitcast.196, s32[1024]{0:T(1024)S(1)} %bitcast.197), kind=kCustom, calls=%fused_computation.37.clone.1 | custom fusion | flops 786432 | bytes 4203008 | tf_op jit(solution)/shard_map/while/body/eval_jaxpr/scatter-add | solution.py:160
  608.5 10.8 %scatter_custom_fusion.6 = f32[4096,256]{1,0:T(8,128)} fusion(f32[4096,256]{1,0:T(8,128)} %get-tuple-element.564, s32[1024]{0:T(1024)S(1)} %bitcast.199, f32[]{:T(128)} %constant.115.clone.1..sunk, f32[1024]{0:T(1024)S(1)} %bitcast.196, s32[1024]{0:T(1024)S(1)} %bitcast.197), kind=kCustom, calls=%fused_computation.37.clone.1 | custom fusion | flops 786432 | bytes 4203008 | tf_op jit(solution)/shard_map/while/body/eval_jaxpr/scatter-add | solution.py:160
  624.0 9.3 %fusion.32 = f32[1,16,256,256]{3,2,1,0:T(8,128)} fusion(f32[4,16,64,256]{3,2,0,1:T(8,128)S(1)} %copy.34, f32[16,256,256]{2,1,0:T(8,128)S(1)} %copy-done.3, f32[16]{0:T(128)S(1)} %dynamic-slice_multiply_fusion, f32[256,256]{1,0:T(8,128)S(1)} %copy-done.7, f32[1,16,256,256]{3,2,1,0:T(8,128)S(1)} %bitcast.180), kind=kOutput, calls=%fused_computation.75 | convolution fusion | flops 3224371200 | bytes 17039424 | tf_op jit(solution)/shard_map/lxb,yb->lxy/dot_general | solution.py:74
  633.4 5.0 add_bitcast_fusion
  (260 shorter events, 169.5 us)
Async XLA Ops:
  0.6 554.8 %copy-start = (f32[256,256]{1,0:T(8,128)S(1)}, f32[256,256]{1,0:T(8,128)}, u32[]{:S(2)}) copy-start(f32[256,256]{1,0:T(8,128)} %param.31) | copy-start | bytes 786436
  0.6 95.1 %collective-permute-start = (f32[16,256,256]{2,1,0:T(8,128)}, f32[16,256,256]{2,1,0:T(8,128)}, u32[]{:S(2)}, u32[]{:S(2)}) collective-permute-start(f32[16,256,256]{2,1,0:T(8,128)} %bitcast.178), channel_id=1, source_target_pairs={{0,4},{4,8},{8,12},{12,16},{16,20},{20,24},{24,28},{1,5},{5,9},{9,... | collective-permute-start | bytes 12582920 | tf_op jit(solution)/shard_map/ppermute | solution.py:15
  14.2 5.3 copy-start.12
  14.2 5.4 copy-start.13
  14.2 5.4 copy-start.14
  14.2 108.5 %all-to-all-start.1 = ((f32[16,256,256]{2,0,1:T(8,128)}), f32[16,256,256]{2,0,1:T(8,128)}, u32[]{:S(2)}, u32[]{:S(2)}) async-start(f32[16,256,256]{2,0,1:T(8,128)} %copy.32), calls=%async_computation.1 | async-start | bytes 8388608 | tf_op jit(solution)/shard_map/all_to_all | solution.py:118
  122.7 53.7 %all-to-all-start = ((f32[16,256,256]{2,0,1:T(8,128)}), f32[16,256,256]{2,0,1:T(8,128)}, u32[]{:S(2)}, u32[]{:S(2)}) async-start(f32[16,256,256]{2,0,1:T(8,128)} %copy.30), calls=%async_computation | async-start | bytes 8388608 | tf_op jit(solution)/shard_map/all_to_all | solution.py:117
  183.0 5.1 copy-start.5
  183.0 5.1 copy-start.6
  183.0 5.1 copy-start.11
  429.9 5.0 copy-start.8
  429.9 53.2 %all-to-all-start.3 = ((f32[64,64,256]{2,1,0:T(8,128)}), f32[64,64,256]{2,1,0:T(8,128)}, u32[]{:S(2)}, u32[]{:S(2)}) async-start(f32[64,64,256]{2,1,0:T(8,128)} %get-tuple-element.301), calls=%async_computation.3 | async-start | bytes 8388608 | tf_op jit(solution)/shard_map/all_to_all | solution.py:125
  483.1 136.2 %all-to-all-start.2 = ((f32[64,64,256]{2,1,0:T(8,128)}), f32[64,64,256]{2,1,0:T(8,128)}, u32[]{:S(2)}, u32[]{:S(2)}) async-start(f32[64,64,256]{2,1,0:T(8,128)} %get-tuple-element.299), calls=%async_computation.2 | async-start | bytes 8388608 | tf_op jit(solution)/shard_map/all_to_all | solution.py:124
  507.4 125.9 %collective-permute-start.1 = (f32[16,256,256]{2,1,0:T(8,128)}, f32[16,256,256]{2,1,0:T(8,128)}, u32[]{:S(2)}, u32[]{:S(2)}) collective-permute-start(f32[16,256,256]{2,1,0:T(8,128)} %multiply_subtract_fusion), channel_id=1, source_target_pairs={{4,0},{8,4},{12,8},{16,12},{20,16},{24,20},{28,24},{5,1},{9,5},{13... | collective-permute-start | bytes 12582920 | tf_op jit(solution)/shard_map/ppermute | solution.py:15
  508.7 25.4 %copy-start.9 = (f32[1,1024]{1,0:T(1,128)S(1)}, f32[1,1024]{1,0:T(1,128)}, u32[]{:S(2)}) copy-start(f32[1,1024]{1,0:T(1,128)} %param.23) | copy-start | bytes 12292
  508.7 31.9 %copy-start.10 = (f32[1,1024]{1,0:T(1,128)S(1)}, f32[1,1024]{1,0:T(1,128)}, u32[]{:S(2)}) copy-start(f32[1,1024]{1,0:T(1,128)} %param.25) | copy-start | bytes 12292
  508.8 31.9 %copy-start.16 = (u32[32]{0:T(128)S(1)}, u32[32]{0:T(128)}, u32[]{:S(2)}) copy-start(u32[32]{0:T(128)} %constant.160) | copy-start | bytes 388
  508.8 46.0 %copy-start.15 = (f32[64]{0:T(128)S(1)}, f32[64]{0:T(128)}, u32[]{:S(2)}) copy-start(f32[64]{0:T(128)} %param.30) | copy-start | bytes 772
  555.4 8.8 %copy-start.7 = (f32[256,256]{1,0:T(8,128)S(1)}, f32[256,256]{1,0:T(8,128)}, u32[]{:S(2)}) copy-start(f32[256,256]{1,0:T(8,128)} %param.32) | copy-start | bytes 786436
  619.3 3.5 copy-start.1
  619.3 4.7 copy-start.3
  624.0 9.4 %copy-start.2 = (f32[1,16,256,256]{3,2,1,0:T(8,128)S(1)}, f32[1,16,256,256]{3,2,1,0:T(8,128)}, u32[]{:S(2)}) copy-start(f32[1,16,256,256]{3,2,1,0:T(8,128)} %param.22) | copy-start | bytes 12582916
  624.0 9.4 %copy-start.4 = (f32[4096,256]{1,0:T(8,128)S(1)}, f32[4096,256]{1,0:T(8,128)}, u32[]{:S(2)}) copy-start(f32[4096,256]{1,0:T(8,128)} %get-tuple-element.302) | copy-start | bytes 12582916
where the time goes:
time: 648 us; the launch traced here: 639 us
  matrix products  197 us (30%)
  waiting for transfers between devices  166 us (26%)
  local copies, waits for them, and re-layouts  135 us (21%)
  other arithmetic  90.7 us (14%)
  starting transfers between devices  29 us (4%)
  blocking collectives  18.2 us (3%)
    ppermute x2, waiting for transfers between devices, from_behind(): lax.ppermute(value, axis, [(source, source + steps) for source in range(f...  76 us
    dot_general x16, matrix products, visit(): jnp.dot(layer_in, path, preferred_element_type=jnp.float32)  58.1 us
    dot_general x16, matrix products, visit(): jnp.dot(layer_out, hidden, preferred_element_type=jnp.float32)  55.8 us
    dot_general x16, matrix products, visit(): jnp.dot(layer_in.T, back_hidden, preferred_element_type=jnp.float32)  55.8 us
    dynamic_slice x48, local copies, waits for them, and re-layouts, select(): piece = lax.dynamic_slice_in_dim(source, first_row, block_rows, 1)  51.3 us
    all_to_all x1, waiting for transfers between devices, body(): lax.all_to_all(backward, 'space', split_axis=0, concat_axis=1, tiled=True)  48.1 us
    scatter-add x4, other arithmetic, add_block(): return total.at[block_rows_index].add(spread_rows, mode='drop')  43 us
    all_to_all x1, waiting for transfers between devices, body(): lax.all_to_all(outgoing, 'space', split_axis=1, concat_axis=0, tiled=True)  41.6 us
  transfers between devices with their start and end apart: 6, of which 3 were waited for; matrix products, arithmetic and copies ran while one was open for 25% of the time, Pallas kernels for 0%

commit v1 on v0

v1 whole, which is shorter than its diff:
```python
import functools

import jax
import jax.numpy as jnp
from jax import lax
from jax.experimental import pallas as pl
from jax.experimental.pallas import tpu as pltpu
from jax.sharding import PartitionSpec as P

STEPS = 4
BIAS_TERMS = 3
BIAS_PAD = 16

exact_mode = lax.Precision.HIGHEST
MIB = 2**20


def partner(index, turn, count):
    if count & (count - 1) == 0:
        return index ^ turn
    return lax.rem(turn - index + count, count)


def send(value, turn, shift):
    windows, count = lax.axis_size("win"), lax.axis_size("space")
    pairs = []
    for window in range(max(0, -shift), min(windows, windows - shift)):
        for index in range(count):
            other = index ^ turn if count & (count - 1) == 0 else (turn - index) % count
            pairs.append((window * count + index, (window + shift) * count + other))
    if all(source == target for source, target in pairs):
        return value
    return lax.ppermute(value, ("win", "space"), pairs)


def full_spec(array):
    return pl.BlockSpec(array.shape, lambda *_: (0,) * array.ndim)


def four_steps(field, other, weights, rows, cols):
    keep, row_up, row_down, col_up, col_down = weights
    lane = lax.broadcasted_iota(jnp.int32, (rows, cols), 1)
    source, target = field, other
    result = None
    for step in range(STEPS):
        centre = source[8 : 8 + rows, :]
        up = source[9 : 9 + rows, :]
        down = source[7 : 7 + rows, :]
        right = jnp.where(lane == cols - 1, 0.0, pltpu.roll(centre, cols - 1, 1))
        left = jnp.where(lane == 0, 0.0, pltpu.roll(centre, 1, 1))
        result = keep * centre + row_up * up + row_down * down + col_up * right + col_down * left
        if step < STEPS - 1:
            target[8 : 8 + rows, :] = result
            source, target = target, source
    return result


def clear_edges(rows, cols, *fields):
    for field in fields:
        field[0:8, :] = jnp.zeros((8, cols), jnp.float32)
        field[8 + rows : 16 + rows, :] = jnp.zeros((8, cols), jnp.float32)


def out_kernel(count, rows, cols, place, weights, field, *refs):
    strips, (work, other) = refs[:count], refs[count:]
    level = pl.program_id(0)

    @pl.when(level == 0)
    def _():
        clear_edges(rows, cols, work, other)

    work[8 : 8 + rows, :] = field[0]
    scalars = [weights[term, level] for term in range(5)]
    work[8 : 8 + rows, :] = four_steps(work, other, scalars, rows, cols)
    height = rows // count
    for turn in range(count):
        start = pl.multiple_of(8 + place[turn] * height, 8)
        strips[turn][0] = work[pl.ds(start, height), :]


def stencil_out(field, weights, place):
    levels, rows, cols = field.shape
    count = place.shape[0]
    height = rows // count
    return pl.pallas_call(
        functools.partial(out_kernel, count, rows, cols),
        grid_spec=pltpu.PrefetchScalarGridSpec(
            num_scalar_prefetch=2,
            grid=(levels,),
            in_specs=[pl.BlockSpec((1, rows, cols), lambda level, *_: (level, 0, 0))],
            out_specs=[pl.BlockSpec((1, height, cols), lambda level, *_: (level, 0, 0))] * count,
            scratch_shapes=[pltpu.VMEM((rows + 16, cols), jnp.float32)] * 2,
        ),
        out_shape=[jax.ShapeDtypeStruct((levels, height, cols), jnp.float32)] * count,
        cost_estimate=pl.CostEstimate(
            flops=STEPS * 20 * field.size, bytes_accessed=8 * field.size, transcendentals=0
        ),
        name="stencil_out",
    )(place, weights, field)


def in_kernel(count, rows, cols, place, weights, *refs):
    strips, base, out = refs[:count], refs[count], refs[count + 1]
    work, other = refs[count + 2 :]
    level = pl.program_id(0)

    @pl.when(level == 0)
    def _():
        clear_edges(rows, cols, work, other)

    height = rows // count
    for turn in range(count):
        start = pl.multiple_of(8 + place[turn] * height, 8)
        work[pl.ds(start, height), :] = strips[turn][0]
    scalars = [weights[term, level] for term in range(5)]
    out[0] = base[0] - four_steps(work, other, scalars, rows, cols)


def stencil_in(strips, base, weights, place):
    levels, rows, cols = base.shape
    count = place.shape[0]
    height = rows // count
    strip_spec = pl.BlockSpec((1, height, cols), lambda level, *_: (level, 0, 0))
    slab_spec = pl.BlockSpec((1, rows, cols), lambda level, *_: (level, 0, 0))
    return pl.pallas_call(
        functools.partial(in_kernel, count, rows, cols),
        grid_spec=pltpu.PrefetchScalarGridSpec(
            num_scalar_prefetch=2,
            grid=(levels,),
            in_specs=[strip_spec] * count + [slab_spec],
            out_specs=slab_spec,
            scratch_shapes=[pltpu.VMEM((rows + 16, cols), jnp.float32)] * 2,
        ),
        out_shape=jax.ShapeDtypeStruct(base.shape, jnp.float32),
        cost_estimate=pl.CostEstimate(
            flops=STEPS * 20 * base.size, bytes_accessed=12 * base.size, transcendentals=0
        ),
        name="stencil_in",
    )(place, weights, *strips, base)


def net_kernel(count, levels, rows, cols, *refs):
    strips = refs[:count]
    path, gate, first, second = refs[count : count + 4]
    outs = refs[count + 4 : 2 * count + 4]
    values, paths, results = refs[2 * count + 4 :]
    for turn in range(count):
        span = slice(turn * levels, (turn + 1) * levels)
        values[:, span, :] = jnp.swapaxes(strips[turn][...], 0, 1)
    paths[...] = jnp.swapaxes(path[...].astype(jnp.float32), 0, 1).astype(jnp.bfloat16)
    term = lax.broadcasted_iota(jnp.int32, (BIAS_PAD, cols), 0)
    ones = jnp.where(term < BIAS_TERMS, 1.0, 0.0).astype(jnp.bfloat16)

    def visit(row, carry):
        centre = values[row]
        half = jnp.dot(
            gate[...], jnp.concatenate([paths[row], ones], 0), preferred_element_type=jnp.float32
        )
        hidden = jnp.dot(first[...], centre.astype(jnp.bfloat16), preferred_element_type=jnp.float32)
        bent = jnp.tanh(half)
        slope = (1.0 + bent) * (1.0 + half * (1.0 - bent))
        hidden = (slope * hidden).astype(jnp.bfloat16)
        results[row] = centre + jnp.dot(second[...], hidden, preferred_element_type=jnp.float32)
        return carry

    lax.fori_loop(0, rows, visit, 0, unroll=2)
    for turn in range(count):
        span = slice(turn * levels, (turn + 1) * levels)
        outs[turn][...] = jnp.swapaxes(results[:, span, :], 0, 1)


def network(strips, path, gate, first, second):
    count = len(strips)
    levels, height, cols = strips[0].shape
    rows = min(16, height)
    total = count * levels
    strip_spec = pl.BlockSpec((levels, rows, cols), lambda step: (0, step, 0))
    return pl.pallas_call(
        functools.partial(net_kernel, count, levels, rows, cols),
        grid=(height // rows,),
        in_specs=[strip_spec] * count
        + [pl.BlockSpec((total, rows, cols), lambda step: (0, step, 0))]
        + [full_spec(gate), full_spec(first), full_spec(second)],
        out_specs=[strip_spec] * count,
        out_shape=[jax.ShapeDtypeStruct(strips[0].shape, jnp.float32)] * count,
        scratch_shapes=[
            pltpu.VMEM((rows, total, cols), jnp.float32),
            pltpu.VMEM((rows, total, cols), jnp.bfloat16),
            pltpu.VMEM((rows, total, cols), jnp.float32),
        ],
        compiler_params=pltpu.CompilerParams(vmem_limit_bytes=40 * MIB),
        cost_estimate=pl.CostEstimate(
            flops=4 * 3 * 2 * height * cols * total * first.shape[0],
            bytes_accessed=10 * total * height * cols,
            transcendentals=height * cols * first.shape[0],
        ),
        name="network",
    )(*strips, path, gate, first, second)


def correlate_kernel(spread, row_factor, col_factor, fields, state, out, rows_pair, cols_pair):
    level = pl.program_id(0)
    same = (((1,), (1,)), ((), ()))

    @pl.when(level == 0)
    def _():
        for pair, factor in ((rows_pair, row_factor), (cols_pair, col_factor)):
            pair[...] = lax.dot_general(
                factor[...], factor[...], same, precision=exact_mode,
                preferred_element_type=jnp.float32,
            )

    inner = jnp.dot(
        fields[0], cols_pair[...], precision=exact_mode, preferred_element_type=jnp.float32
    )
    outer = jnp.dot(
        rows_pair[...], inner, precision=exact_mode, preferred_element_type=jnp.float32
    )
    scale = spread[level] * spread[level]
    out[0] = scale * outer + state[0]


def correlate(fields, state, spread, row_factor, col_factor):
    levels, rows, cols = fields.shape
    slab_spec = pl.BlockSpec((1, rows, cols), lambda level, *_: (level, 0, 0))
    return pl.pallas_call(
        correlate_kernel,
        grid_spec=pltpu.PrefetchScalarGridSpec(
            num_scalar_prefetch=1,
            grid=(levels,),
            in_specs=[full_spec(row_factor), full_spec(col_factor), slab_spec, slab_spec],
            out_specs=slab_spec,
            scratch_shapes=[pltpu.VMEM((rows, rows), jnp.float32), pltpu.VMEM((cols, cols), jnp.float32)],
        ),
        out_shape=jax.ShapeDtypeStruct(fields.shape, jnp.float32),
        cost_estimate=pl.CostEstimate(
            flops=6 * 2 * fields.size * (rows + cols), bytes_accessed=12 * fields.size, transcendentals=0
        ),
        name="correlate",
    )(spread, row_factor, col_factor, fields, state)


def combine_kernel(place, whole, strip, out):
    out[...] = whole[...] - strip[...]


def combine(whole, strips, place):
    levels, rows, cols = whole.shape
    count = place.shape[0]
    height = rows // count
    for turn in range(count):
        block = pl.BlockSpec(
            (levels, height, cols), lambda step, place, turn=turn: (0, place[turn], 0)
        )
        strip_spec = pl.BlockSpec((levels, height, cols), lambda step, place: (0, 0, 0))
        whole = pl.pallas_call(
            combine_kernel,
            grid_spec=pltpu.PrefetchScalarGridSpec(
                num_scalar_prefetch=1,
                grid=(1,),
                in_specs=[block, strip_spec],
                out_specs=block,
            ),
            out_shape=jax.ShapeDtypeStruct(whole.shape, jnp.float32),
            input_output_aliases={1: 0},
            cost_estimate=pl.CostEstimate(
                flops=strips[turn].size, bytes_accessed=12 * strips[turn].size, transcendentals=0
            ),
            name="combine",
        )(place, whole, strips[turn])
    return whole


def observe_kernel(group, row_index, col_index, duals, state, mult, base, seen, picked):
    count = picked.shape[0]
    base[...] = mult[...]
    lane = lax.broadcasted_iota(jnp.int32, (1, state.shape[1]), 1)
    spot = lax.broadcasted_iota(jnp.int32, (8, 128), 0) * 128 + lax.broadcasted_iota(
        jnp.int32, (8, 128), 1
    )

    def visit(block, carry):
        for item in range(group):
            index = block * group + item
            row, col = row_index[index], col_index[index]
            found = jnp.where(lane == col, state[pl.ds(row, 1), :], 0.0)
            total = found[:, 0:128]
            for first in range(128, state.shape[1], 128):
                total = total + found[:, first : first + 128]
            picked[pl.ds(index, 1), :] = total
            top = pl.multiple_of((row >> 3) << 3, 8)
            side = pl.multiple_of(jnp.maximum((col >> 7) << 7, 0), 128)
            tile = (pl.ds(top, 8), pl.ds(side, 128))
            hit = spot == jnp.where(col < 0, -1, ((row & 7) << 7) + (col & 127))
            base[tile] = base[tile] + jnp.where(hit, duals[index], 0.0)
        return carry

    lax.fori_loop(0, count // group, visit, 0)
    ones = jnp.ones((8, 128), jnp.float32)
    seen[...] = lax.dot_general(
        ones, picked[...], (((1,), (1,)), ((), ())), precision=exact_mode,
        preferred_element_type=jnp.float32,
    )


def observe(row_index, col_index, duals, state, mult):
    count = duals.shape[0]
    vmem = pl.BlockSpec(memory_space=pltpu.VMEM)
    smem = pl.BlockSpec(memory_space=pltpu.SMEM)
    base, seen = pl.pallas_call(
        functools.partial(observe_kernel, 8),
        in_specs=[smem, smem, smem, vmem, vmem],
        out_specs=[vmem, vmem],
        out_shape=[
            jax.ShapeDtypeStruct(mult.shape, jnp.float32),
            jax.ShapeDtypeStruct((8, count), jnp.float32),
        ],
        scratch_shapes=[pltpu.VMEM((count, 128), jnp.float32)],
        compiler_params=pltpu.CompilerParams(vmem_limit_bytes=40 * MIB),
        cost_estimate=pl.CostEstimate(
            flops=20000 * count, bytes_accessed=12 * mult.size, transcendentals=0
        ),
        name="observe",
    )(row_index, col_index, duals, state, mult)
    return base, seen[0]


def bias_terms(bias):
    terms, rest = [], bias
    for _ in range(BIAS_TERMS):
        term = lax.reduce_precision(rest, 8, 7)
        terms.append(term.astype(jnp.bfloat16))
        rest = rest - term
    zero = jnp.zeros((bias.shape[0], BIAS_PAD - BIAS_TERMS), jnp.bfloat16)
    return jnp.concatenate([jnp.stack(terms, 1), zero], 1)


def body(
    increment,
    multiplier,
    obs_dual,
    obs_sites,
    obs_variance,
    trajectory,
    diffusion,
    drift_rows,
    drift_cols,
    spread,
    row_factor,
    col_factor,
    layer_in,
    bias_in,
    layer_out,
):
    state, mult, path = increment[0], multiplier[0], trajectory[0]
    levels, rows, cols = state.shape
    count = lax.axis_size("space")
    here = lax.axis_index("space")
    height = rows // count
    first_level = here * levels
    turns = range(count)
    place = jnp.stack([partner(here, turn, count) for turn in turns]).astype(jnp.int32)

    def local(values):
        return lax.dynamic_slice_in_dim(values, first_level, levels)

    def weights(direction):
        mix, along, across = local(diffusion), direction * local(drift_rows), direction * local(drift_cols)
        return jnp.stack([1.0 - 4.0 * mix, mix - along, mix + along, mix - across, mix + across])

    mult_strips = [
        send(lax.dynamic_slice_in_dim(mult, place[turn] * height, height, 1), turn, 0) for turn in turns
    ]
    stepped = stencil_out(state, weights(1.0), place)
    state_strips = [send(stepped[turn], turn, 1) for turn in turns]

    half = jnp.asarray(0.5, jnp.bfloat16)
    gate = jnp.concatenate([layer_in, bias_terms(bias_in)], 1) * half
    columns = (place[:, None] * levels + jnp.arange(levels, dtype=jnp.int32)[None, :]).reshape(-1)
    layer_in_own = jnp.take(layer_in, columns, axis=1)
    layer_out_own = jnp.take(layer_out, columns, axis=0)

    partial = correlate(mult, state, local(spread), row_factor, col_factor)

    owned = obs_dual.shape[1]
    positions = obs_sites[0]
    all_duals = [send(obs_dual[0], turn, 0) for turn in turns]
    duals = jnp.concatenate(all_duals)
    ordered = jnp.take(positions.reshape(3, count, owned), place, axis=1).reshape(3, -1)
    local_level = ordered[0] - first_level
    inside = (local_level >= 0) & (local_level < levels)
    row_index = jnp.where(inside, local_level * rows + ordered[1], 0)
    col_index = jnp.where(inside, ordered[2], -1)
    base, seen = observe(
        row_index, col_index, duals, state.reshape(-1, cols), mult.reshape(-1, cols)
    )
    base = base.reshape(mult.shape)
    parts = [send(seen[turn * owned : (turn + 1) * owned], turn, 0) for turn in turns]
    obs_out = obs_variance[0] * obs_dual[0] + sum(parts[1:], parts[0])

    adjoint = network(mult_strips, path, gate, layer_out_own.T, layer_in_own.T * half)
    adjoint_strips = [send(adjoint[turn], turn, -1) for turn in turns]
    tangent = network(state_strips, path, gate, layer_in_own, layer_out_own * half)
    tangent_strips = [send(tangent[turn], turn, 0) for turn in turns]

    state_out = combine(partial, tangent_strips, place)
    mult_out = stencil_in(adjoint_strips, base, weights(-1.0), place)
    return (state_out[None], obs_out[None], mult_out[None])


def solution(mesh):
    placed = (
        P("win", "space", None, None),
        P("win", "space", None, None),
        P("win", "space"),
        P("win", None, None),
        P("win", "space"),
        P("win", None, "space", None),
        P(),
        P(),
        P(),
        P(),
        P(),
        P(),
        P(),
        P(),
        P(),
    )
    return jax.shard_map(
        body,
        mesh=mesh,
        in_specs=placed,
        out_specs=(P("win", "space", None, None), P("win", "space"), P("win", "space", None, None)),
        check_vma=False,
    )
```

time: 648 us -> 320 us (0.49); the launches traced: 639 us -> 318 us
  matrix products: 197 us -> 0 us
  Pallas kernels: 0 us -> 175 us
  local copies, waits for them, and re-layouts: 135 us -> 18.1 us
  other arithmetic: 90.7 us -> 3.4 us
  waiting for transfers between devices: 166 us -> 90.5 us
  blocking collectives: 18.2 us -> 0 us
    dot_general x52 -> x0, matrix products: 197 us -> none  [the longest x16 58.1 us: visit(): jnp.dot(layer_in, path, preferred_element_type=jnp.float32)]
    pallas_call x0 -> x10, Pallas kernels: none -> 175 us  [the longest x2 71.7 us: network(): pl.pallas_call(functools.partial(net_kernel, count, levels, rows, cols),...]
    all_to_all x4 -> x0, waiting for transfers between devices: 89.7 us -> none  [the longest x1 48.1 us: body(): lax.all_to_all(backward, 'space', split_axis=0, concat_axis=1, tiled=True)]
    dynamic_slice x63 -> x2, local copies, waits for them, and re-layouts: 51.7 us -> 4.61 us  [the longest x1 4.02 us: body(): lax.dynamic_slice_in_dim(mult, place[turn] * height, height, 1)]
    scatter-add x4 -> x0, other arithmetic: 43 us -> none  [add_block(): return total.at[block_rows_index].add(spread_rows, mode='drop')]
    sub x8 -> x0, other arithmetic: 39 us -> none  [stencil_step(): return centre + diffusion * mixing - direction * carried]
    ppermute x2 -> x20, starting transfers between devices: 8.25 us -> 30 us  [send(): return lax.ppermute(value, ('win', 'space'), pairs)]
    all_to_all x4 -> x0, starting transfers between devices: 20.7 us -> none  [the longest x1 5.46 us: body(): lax.all_to_all(outgoing, 'space', split_axis=1, concat_axis=0, tiled=True)]
  transfers between devices with their start and end apart: 6 -> 20, of which waited for: 3 -> 3; matrix products, arithmetic and copies ran while one was open for 25% -> 4% of each run, Pallas kernels for 0% -> 49%
where the time goes in v1:
time: 320 us; the launch traced here: 318 us
  Pallas kernels  175 us (55%)
  waiting for transfers between devices  90.5 us (28%)
  starting transfers between devices  30 us (9%)
  local copies, waits for them, and re-layouts  18.1 us (6%)
  other arithmetic  3.4 us (1%)
    ppermute x20, waiting for transfers between devices, send(): return lax.ppermute(value, ('win', 'space'), pairs)  90.5 us
    pallas_call x2, Pallas kernels, network(): pl.pallas_call(functools.partial(net_kernel, count, levels, rows, cols),...  71.7 us
    pallas_call x1, Pallas kernels, observe(): pl.pallas_call(functools.partial(observe_kernel, 8), in_specs=[smem, smem...  33.2 us
    ppermute x20, starting transfers between devices, send(): return lax.ppermute(value, ('win', 'space'), pairs)  30 us
    pallas_call x1, Pallas kernels, correlate(): pl.pallas_call(correlate_kernel, grid_spec=pltpu.PrefetchScalarGridSpec(n...  20.9 us
    pallas_call x1, Pallas kernels, stencil_in(): pl.pallas_call(functools.partial(in_kernel, count, rows, cols), grid_spec...  18.6 us
    pallas_call x1, Pallas kernels, stencil_out(): pl.pallas_call(functools.partial(out_kernel, count, rows, cols), grid_spe...  17.4 us
    pallas_call x4, Pallas kernels, combine(): pl.pallas_call(combine_kernel, grid_spec=pltpu.PrefetchScalarGridSpec(num...  13.3 us
  transfers between devices with their start and end apart: 20, of which 3 were waited for; matrix products, arithmetic and copies ran while one was open for 4% of the time, Pallas kernels for 49%

profile of v1, /device:TPU:0, one launch (start us, length us, event | category | flops | bytes accessed | tf_op | source)
XLA Modules:
  0.0 318.2 jit_solution(11124794729623662168)
XLA Ops:
  0.6 0.0 copy-start
  0.7 2.4 collective-permute-start.9
  3.1 0.7 add_bitcast_fusion
  3.9 0.7 subtract_bitcast_fusion
  4.6 0.7 compare_and_fusion.1
  5.3 0.6 stack.78.weights
  5.9 17.4 %stencil_out.1 = (f32[16,64,256]{2,1,0:T(8,128)}, f32[16,64,256]{2,1,0:T(8,128)}, f32[16,64,256]{2,1,0:T(8,128)}, f32[16,64,256]{2,1,0:T(8,128)}) custom-call(s32[4]{0:T(128)} %get-tuple-element.39.place, f32[5,16]{1,0:T(8,128)} %stack.78.weights, f32[16,256,256]{2,1,0:T(8,128)} %bitcast.67), custom_call_target="tpu_custom_call" | custom-call | flops 83886080 | bytes 8388608 | tf_op jit(solution)/shard_map/stencil_out/pallas_call | solution.py:85
  23.3 3.6 %collective-permute-start = (f32[16,64,256]{2,1,0:T(8,128)}, f32[16,64,256]{2,1,0:T(8,128)S(1)}, u32[]{:S(2)}, u32[]{:S(2)}) collective-permute-start(f32[16,64,256]{2,1,0:T(8,128)} %get-tuple-element.17), channel_id=1, source_target_pairs={{0,4},{1,5},{2,6},{3,7},{4,8},{5,9},{6,10},{7,11},{8,12},{9,13},{1... | collective-permute-start | bytes 3145736 | tf_op jit(solution)/shard_map/ppermute | solution.py:33
  26.9 4.4 %collective-permute-start.1 = (f32[16,64,256]{2,1,0:T(8,128)}, f32[16,64,256]{2,1,0:T(8,128)}, u32[]{:S(2)}, u32[]{:S(2)}) collective-permute-start(f32[16,64,256]{2,1,0:T(8,128)} %get-tuple-element.18), channel_id=1, source_target_pairs={{0,5},{1,4},{2,7},{3,6},{4,9},{5,8},{6,11},{7,10},{8,13},{9,12},{1... | collective-permute-start | bytes 3145736 | tf_op jit(solution)/shard_map/ppermute | solution.py:33
  31.3 3.4 %collective-permute-start.2 = (f32[16,64,256]{2,1,0:T(8,128)}, f32[16,64,256]{2,1,0:T(8,128)}, u32[]{:S(2)}, u32[]{:S(2)}) collective-permute-start(f32[16,64,256]{2,1,0:T(8,128)} %get-tuple-element.19), channel_id=1, source_target_pairs={{0,6},{1,7},{2,4},{3,5},{4,10},{5,11},{6,8},{7,9},{8,14},{9,15},{1... | collective-permute-start | bytes 3145736 | tf_op jit(solution)/shard_map/ppermute | solution.py:33
  34.7 3.7 %collective-permute-start.3 = (f32[16,64,256]{2,1,0:T(8,128)}, f32[16,64,256]{2,1,0:T(8,128)}, u32[]{:S(2)}, u32[]{:S(2)}) collective-permute-start(f32[16,64,256]{2,1,0:T(8,128)} %get-tuple-element.20), channel_id=1, source_target_pairs={{0,7},{1,6},{2,5},{3,4},{4,11},{5,10},{6,9},{7,8},{8,15},{9,14},{1... | collective-permute-start | bytes 3145736 | tf_op jit(solution)/shard_map/ppermute | solution.py:33
  38.5 0.1 iota_add_fusion
  38.5 0.1 add.127
  38.6 0.1 add.124
  38.8 0.2 copy.31
  38.9 0.7 gather_fusion
  39.7 0.7 gather_fusion.1
  40.4 0.1 multiply_bitcast_fusion
  40.5 0.1 fusion
  40.6 0.2 stack.94
  40.8 0.2 stack.93
  41.0 0.2 stack.92
  41.2 0.6 concatenate.31
  41.9 0.1 fusion.5
  42.0 0.1 reduce
  42.1 0.6 gather_fusion.2
  42.7 0.1 select_bitcast_fusion.1
  42.8 0.7 collective-permute-start.8
  43.5 0.1 slice_select_fusion
  43.6 37.5 %collective-permute-done.8 = f32[1024]{0:T(1024)S(1)} collective-permute-done((f32[1024]{0:T(1024)S(1)}, f32[1024]{0:T(1024)S(1)}, u32[]{:S(2)}, u32[]{:S(2)}) %collective-permute-start.8) | collective-permute-done | bytes 4128 | tf_op jit(solution)/shard_map/ppermute | solution.py:33
  81.1 4.0 %dynamic-slice_bitcast_fusion = (f32[16,64,256]{2,1,0:T(8,128)}, f32[16,64,256]{2,1,0:T(8,128)}, f32[16,64,256]{2,1,0:T(8,128)S(1)}, f32[16,64,256]{2,1,0:T(8,128)}) fusion(f32[1,16,256,256]{3,2,1,0:T(8,128)} %param.16, s32[]{:T(128)S(6)} %select_n.97, s32[]{:T(128)S(6)} %select_n.95, s32[]{:T(128)S(6)} %select_n.94, s32[]{:T(128)S(6)} %select_n.96), kind=kLoop, calls=%fused_computation.3 | loop fusion | bytes 8388624 | tf_op jit(solution)/shard_map/dynamic_slice | solution.py:372
  85.1 0.2 copy.37.refs_6_
  85.3 0.2 copy.35.refs_6_
  85.5 0.8 collective-permute-start.15
  86.3 2.2 copy-done.1
  88.5 2.2 copy-done.2
  90.7 33.2 %observe.1 = (f32[4096,256]{1,0:T(8,128)S(1)}, f32[8,4096]{1,0:T(8,128)S(1)}) custom-call(s32[4096]{0:T(1024)S(1)} %bitcast.72, s32[4096]{0:T(1024)S(1)} %bitcast.71, f32[4096]{0:T(1024)S(1)} %pad_maximum_fusion.duals, f32[4096,256]{1,0:T(8,128)S(1)} %bitcast.69, f32[4096,256]{1,0:T(8,128)S(1)} %bitcast.66), custom_call_target="tpu_custom_call" | custom-call | flops 81920000 | bytes 12582912 | tf_op jit(solution)/shard_map/observe/pallas_call | solution.py:310
  123.9 2.0 copy-done.3
  125.9 0.1 collective-permute-start.13
  126.0 1.5 collective-permute-start.14
  127.5 0.4 collective-permute-start.12
  127.9 0.4 collective-permute-start.10
  128.2 36.2 %network.2 = (f32[16,64,256]{2,1,0:T(8,128)S(1)}, f32[16,64,256]{2,1,0:T(8,128)S(1)}, f32[16,64,256]{2,1,0:T(8,128)S(1)}, f32[16,64,256]{2,1,0:T(8,128)}) custom-call(f32[16,64,256]{2,1,0:T(8,128)S(1)} %collective-permute-done.refs_0_, f32[16,64,256]{2,1,0:T(8,128)} %collective-permute-done.1.refs_1_, f32[16,64,256]{2,1,0:T(8,128)} %collective-permute-done.2.refs_2_, ...), custom_call_target="tpu_custom_call" | custom-call | flops 25769803776 | bytes 10485760 | tf_op jit(solution)/shard_map/network/pallas_call | solution.py:178
  164.4 1.0 copy-done.4
  165.4 1.4 collective-permute-start.11
  166.8 0.7 collective-permute-start.5
  167.5 35.5 %network.3 = (f32[16,64,256]{2,1,0:T(8,128)}, f32[16,64,256]{2,1,0:T(8,128)}, f32[16,64,256]{2,1,0:T(8,128)}, f32[16,64,256]{2,1,0:T(8,128)S(1)}) custom-call(f32[16,64,256]{2,1,0:T(8,128)S(1)} %get-tuple-element.42.refs_0_, f32[16,64,256]{2,1,0:T(8,128)S(1)} %collective-permute-done.13.refs_1_, f32[16,64,256]{2,1,0:T(8,128)S(1)} %collective-permute-done.14.refs_2_, ...), custom_call_target="tpu_custom_call" | custom-call | flops 25769803776 | bytes 10485760 | tf_op jit(solution)/shard_map/network/pallas_call | solution.py:178
  203.0 1.2 collective-permute-start.6
  204.2 1.3 collective-permute-start.16
  205.5 1.3 collective-permute-start.17
  206.8 1.3 collective-permute-start.18
  208.2 1.5 collective-permute-start.19
  209.7 0.6 dynamic_slice.35.spread
  210.3 20.9 %correlate.1.whole = f32[16,256,256]{2,1,0:T(8,128)} custom-call(f32[16]{0:T(128)} %dynamic_slice.35.spread, f32[256,256]{1,0:T(8,128)} %row_factor.1, f32[256,256]{1,0:T(8,128)} %col_factor.1, f32[16,256,256]{2,1,0:T(8,128)} %bitcast.65, f32[16,256,256]{2,1,0:T(8,128)} %bitcast.68), custom_call_target="tpu_custom_call" | custom-call | flops 6442450944 | bytes 12582912 | tf_op jit(solution)/shard_map/correlate/pallas_call | solution.py:226
  231.2 3.3 %combine.4.whole = f32[16,256,256]{2,1,0:T(8,128)} custom-call(s32[4]{0:T(128)} %get-tuple-element.39.place, f32[16,256,256]{2,1,0:T(8,128)} %correlate.1.whole, f32[16,64,256]{2,1,0:T(8,128)} %copy-done.4), custom_call_target="tpu_custom_call", output_to_operand_aliasing={{}: (1, {})} | custom-call | flops 262144 | bytes 3145728 | tf_op jit(solution)/shard_map/combine/pallas_call | solution.py:256
  234.4 0.6 stack.91.weights
  235.0 3.4 %combine.5.whole = f32[16,256,256]{2,1,0:T(8,128)} custom-call(s32[4]{0:T(128)} %get-tuple-element.39.place, f32[16,256,256]{2,1,0:T(8,128)} %combine.4.whole, f32[16,64,256]{2,1,0:T(8,128)} %copy-done.10), custom_call_target="tpu_custom_call", output_to_operand_aliasing={{}: (1, {})} | custom-call | flops 262144 | bytes 3145728 | tf_op jit(solution)/shard_map/combine/pallas_call | solution.py:256
  238.5 0.6 add_add_fusion
  239.1 3.3 %combine.6.whole = f32[16,256,256]{2,1,0:T(8,128)} custom-call(s32[4]{0:T(128)} %get-tuple-element.39.place, f32[16,256,256]{2,1,0:T(8,128)} %combine.5.whole, f32[16,64,256]{2,1,0:T(8,128)} %copy-done.9), custom_call_target="tpu_custom_call", output_to_operand_aliasing={{}: (1, {})} | custom-call | flops 262144 | bytes 3145728 | tf_op jit(solution)/shard_map/combine/pallas_call | solution.py:256
  242.4 3.3 %combine.7 = f32[16,256,256]{2,1,0:T(8,128)} custom-call(s32[4]{0:T(128)} %get-tuple-element.39.place, f32[16,256,256]{2,1,0:T(8,128)} %combine.6.whole, f32[16,64,256]{2,1,0:T(8,128)} %collective-permute-done.6.strip), custom_call_target="tpu_custom_call", output_to_operand_aliasing={{}: (1, {})} | custom-call | flops 262144 | bytes 3145728 | tf_op jit(solution)/shard_map/combine/pallas_call | solution.py:256
  245.6 31.6 %collective-permute-done.16.refs_0_ = f32[16,64,256]{2,1,0:T(8,128)S(1)} collective-permute-done((f32[16,64,256]{2,1,0:T(8,128)}, f32[16,64,256]{2,1,0:T(8,128)S(1)}, u32[]{:S(2)}, u32[]{:S(2)}) %collective-permute-start.16) | collective-permute-done | bytes 1048608 | tf_op jit(solution)/shard_map/ppermute | solution.py:33
  277.2 21.3 %collective-permute-done.17.refs_1_ = f32[16,64,256]{2,1,0:T(8,128)S(1)} collective-permute-done((f32[16,64,256]{2,1,0:T(8,128)}, f32[16,64,256]{2,1,0:T(8,128)S(1)}, u32[]{:S(2)}, u32[]{:S(2)}) %collective-permute-start.17) | collective-permute-done | bytes 1048608 | tf_op jit(solution)/shard_map/ppermute | solution.py:33
  298.6 1.0 copy-done.12
  299.5 18.6 %stencil_in.1 = f32[16,256,256]{2,1,0:T(8,128)} custom-call(s32[4]{0:T(128)} %get-tuple-element.39.place, f32[5,16]{1,0:T(8,128)} %stack.91.weights, f32[16,64,256]{2,1,0:T(8,128)} %copy-done.11, f32[16,64,256]{2,1,0:T(8,128)} %copy-done.12, f32[16,64,256]{2,1,0:T(8,128)} %collective-permute-done.18.refs_2_, f32[16,64,256]{2,1,0:T(8,128)} %collective-permute-done.19.refs_3_, ...), custom_call_target="tpu_custom_call" | custom-call | flops 83886080 | bytes 12582912 | tf_op jit(solution)/shard_map/stencil_in/pallas_call | solution.py:125
  (62 shorter events, 0.2 us)
Async XLA Ops:
  0.6 39.0 %copy-start = (bf16[64,1024]{1,0:T(8,128)(2,1)S(1)}, bf16[64,1024]{1,0:T(8,128)(2,1)}, u32[]{:S(2)}) copy-start(bf16[64,1024]{1,0:T(8,128)(2,1)} %param.29) | copy-start | bytes 393220
  0.6 38.1 %copy-start.17 = (f32[1024]{0:T(1024)S(1)}, f32[1024]{0:T(1024)}, u32[]{:S(2)}) copy-start(f32[1024]{0:T(1024)} %param.28) | copy-start | bytes 12292
  0.7 38.1 %copy-start.6 = (bf16[1024,64]{0,1:T(8,128)(2,1)S(1)}, bf16[1024,64]{0,1:T(8,128)(2,1)}, u32[]{:S(2)}) copy-start(bf16[1024,64]{0,1:T(8,128)(2,1)} %param.27) | copy-start | bytes 393220
  0.7 42.1 %collective-permute-start.9 = (f32[1024]{0:T(1024)}, f32[1024]{0:T(1024)S(1)}, u32[]{:S(2)}, u32[]{:S(2)}) collective-permute-start(f32[1024]{0:T(1024)} %bitcast.78), channel_id=1, source_target_pairs={{0,3},{1,2},{2,1},{3,0},{4,7},{5,6},{6,5},{7,4},{8,11},{9,10},{10,... | collective-permute-start | bytes 12296 | tf_op jit(solution)/shard_map/ppermute | solution.py:33
  5.2 33.2 %copy-start.14 = (s32[4]{0:T(128)S(1)}, s32[4]{0:T(128)}, u32[]{:S(2)}) copy-start(s32[4]{0:T(128)} %get-tuple-element.39.place) | copy-start | bytes 52
  23.3 18.7 %copy-start.13 = (s32[1,3,4096]{2,0,1:T(1,128)S(1)}, s32[1,3,4096]{2,0,1:T(1,128)}, u32[]{:S(2)}) copy-start(s32[1,3,4096]{2,0,1:T(1,128)} %param.18) | copy-start | bytes 147460
  23.3 19.6 %copy-start.15 = (f32[1,1024]{1,0:T(1,128)S(1)}, f32[1,1024]{1,0:T(1,128)}, u32[]{:S(2)}) copy-start(f32[1,1024]{1,0:T(1,128)} %param.17) | copy-start | bytes 12292
  23.3 102.6 %collective-permute-start = (f32[16,64,256]{2,1,0:T(8,128)}, f32[16,64,256]{2,1,0:T(8,128)S(1)}, u32[]{:S(2)}, u32[]{:S(2)}) collective-permute-start(f32[16,64,256]{2,1,0:T(8,128)} %get-tuple-element.17), channel_id=1, source_target_pairs={{0,4},{1,5},{2,6},{3,7},{4,8},{5,9},{6,10},{7,11},{8,12},{9,13},{1... | collective-permute-start | bytes 3145736 | tf_op jit(solution)/shard_map/ppermute | solution.py:33
  26.9 99.1 %collective-permute-start.1 = (f32[16,64,256]{2,1,0:T(8,128)}, f32[16,64,256]{2,1,0:T(8,128)}, u32[]{:S(2)}, u32[]{:S(2)}) collective-permute-start(f32[16,64,256]{2,1,0:T(8,128)} %get-tuple-element.18), channel_id=1, source_target_pairs={{0,5},{1,4},{2,7},{3,6},{4,9},{5,8},{6,11},{7,10},{8,13},{9,12},{1... | collective-permute-start | bytes 3145736 | tf_op jit(solution)/shard_map/ppermute | solution.py:33
  31.3 96.2 %collective-permute-start.2 = (f32[16,64,256]{2,1,0:T(8,128)}, f32[16,64,256]{2,1,0:T(8,128)}, u32[]{:S(2)}, u32[]{:S(2)}) collective-permute-start(f32[16,64,256]{2,1,0:T(8,128)} %get-tuple-element.19), channel_id=1, source_target_pairs={{0,6},{1,7},{2,4},{3,5},{4,10},{5,11},{6,8},{7,9},{8,14},{9,15},{1... | collective-permute-start | bytes 3145736 | tf_op jit(solution)/shard_map/ppermute | solution.py:33
  34.7 93.2 %collective-permute-start.3 = (f32[16,64,256]{2,1,0:T(8,128)}, f32[16,64,256]{2,1,0:T(8,128)}, u32[]{:S(2)}, u32[]{:S(2)}) collective-permute-start(f32[16,64,256]{2,1,0:T(8,128)} %get-tuple-element.20), channel_id=1, source_target_pairs={{0,7},{1,6},{2,5},{3,4},{4,11},{5,10},{6,9},{7,8},{8,15},{9,14},{1... | collective-permute-start | bytes 3145736 | tf_op jit(solution)/shard_map/ppermute | solution.py:33
  42.8 38.3 %collective-permute-start.8 = (f32[1024]{0:T(1024)S(1)}, f32[1024]{0:T(1024)S(1)}, u32[]{:S(2)}, u32[]{:S(2)}) collective-permute-start(f32[1024]{0:T(1024)S(1)} %bitcast.79), channel_id=1, source_target_pairs={{0,2},{1,3},{2,0},{3,1},{4,6},{5,7},{6,4},{7,5},{8,10},{9,11},{10,... | collective-permute-start | bytes 12296 | tf_op jit(solution)/shard_map/ppermute | solution.py:33
  81.1 4.4 %collective-permute-start.7 = (f32[1024]{0:T(1024)S(1)}, f32[1024]{0:T(1024)S(1)}, u32[]{:S(2)}, u32[]{:S(2)}) collective-permute-start(f32[1024]{0:T(1024)S(1)} %bitcast.80), channel_id=1, source_target_pairs={{0,1},{1,0},{2,3},{3,2},{4,5},{5,4},{6,7},{7,6},{8,9},{9,8},{10,11... | collective-permute-start | bytes 12296 | tf_op jit(solution)/shard_map/ppermute | solution.py:33
  85.5 79.9 %collective-permute-start.15 = (f32[16,64,256]{2,1,0:T(8,128)}, f32[16,64,256]{2,1,0:T(8,128)S(1)}, u32[]{:S(2)}, u32[]{:S(2)}) collective-permute-start(f32[16,64,256]{2,1,0:T(8,128)} %get-tuple-element.40), channel_id=1, source_target_pairs={{0,3},{1,2},{2,1},{3,0},{4,7},{5,6},{6,5},{7,4},{8,11},{9,10},{10,... | collective-permute-start | bytes 3145736 | tf_op jit(solution)/shard_map/ppermute | solution.py:33
  86.3 2.2 copy-start.1
  88.5 2.2 copy-start.2
  90.7 35.2 %copy-start.8 = (f32[16,64,256]{2,1,0:T(8,128)S(1)}, f32[16,64,256]{2,1,0:T(8,128)}, u32[]{:S(2)}) copy-start(f32[16,64,256]{2,1,0:T(8,128)} %get-tuple-element.41) | copy-start | bytes 3145732
  90.7 35.3 %copy-start.7 = (f32[16,64,256]{2,1,0:T(8,128)S(1)}, f32[16,64,256]{2,1,0:T(8,128)}, u32[]{:S(2)}) copy-start(f32[16,64,256]{2,1,0:T(8,128)} %get-tuple-element.43) | copy-start | bytes 3145732
  90.7 37.6 %copy-start.5 = (bf16[1,64,64,256]{3,2,1,0:T(8,128)(2,1)S(1)}, bf16[1,64,64,256]{3,2,1,0:T(8,128)(2,1)}, u32[]{:S(2)}) copy-start(bf16[1,64,64,256]{3,2,1,0:T(8,128)(2,1)} %param.20) | copy-start | bytes 6291460
  123.9 2.0 copy-start.3
  125.9 40.9 %collective-permute-start.13 = (f32[16,64,256]{2,1,0:T(8,128)S(1)}, f32[16,64,256]{2,1,0:T(8,128)S(1)}, u32[]{:S(2)}, u32[]{:S(2)}) collective-permute-start(f32[16,64,256]{2,1,0:T(8,128)S(1)} %copy-done.8), channel_id=1, source_target_pairs={{0,1},{1,0},{2,3},{3,2},{4,5},{5,4},{6,7},{7,6},{8,9},{9,8},{10,11... | collective-permute-start | bytes 3145736 | tf_op jit(solution)/shard_map/ppermute | solution.py:33
  126.0 40.8 %collective-permute-start.14 = (f32[16,64,256]{2,1,0:T(8,128)S(1)}, f32[16,64,256]{2,1,0:T(8,128)S(1)}, u32[]{:S(2)}, u32[]{:S(2)}) collective-permute-start(f32[16,64,256]{2,1,0:T(8,128)S(1)} %copy-done.7), channel_id=1, source_target_pairs={{0,2},{1,3},{2,0},{3,1},{4,6},{5,7},{6,4},{7,5},{8,10},{9,11},{10,... | collective-permute-start | bytes 3145736 | tf_op jit(solution)/shard_map/ppermute | solution.py:33
  127.5 75.5 %collective-permute-start.12 = (f32[1024]{0:T(1024)S(1)}, f32[1024]{0:T(1024)S(1)}, u32[]{:S(2)}, u32[]{:S(2)}) collective-permute-start(f32[1024]{0:T(1024)S(1)} %bitcast.88), channel_id=1, source_target_pairs={{0,3},{1,2},{2,1},{3,0},{4,7},{5,6},{6,5},{7,4},{8,11},{9,10},{10,... | collective-permute-start | bytes 12296 | tf_op jit(solution)/shard_map/ppermute | solution.py:33
  127.9 76.3 %collective-permute-start.10 = (f32[1024]{0:T(1024)S(1)}, f32[1024]{0:T(1024)S(1)}, u32[]{:S(2)}, u32[]{:S(2)}) collective-permute-start(f32[1024]{0:T(1024)S(1)} %bitcast.87), channel_id=1, source_target_pairs={{0,1},{1,0},{2,3},{3,2},{4,5},{5,4},{6,7},{7,6},{8,9},{9,8},{10,11... | collective-permute-start | bytes 12296 | tf_op jit(solution)/shard_map/ppermute | solution.py:33
  164.4 1.0 copy-start.4
  165.4 40.1 %collective-permute-start.11 = (f32[1024]{0:T(1024)S(1)}, f32[1024]{0:T(1024)S(1)}, u32[]{:S(2)}, u32[]{:S(2)}) collective-permute-start(f32[1024]{0:T(1024)S(1)} %bitcast.86), channel_id=1, source_target_pairs={{0,2},{1,3},{2,0},{3,1},{4,6},{5,7},{6,4},{7,5},{8,10},{9,11},{10,... | collective-permute-start | bytes 12296 | tf_op jit(solution)/shard_map/ppermute | solution.py:33
  166.8 40.0 %collective-permute-start.4 = (f32[16,64,256]{2,1,0:T(8,128)S(1)}, f32[16,64,256]{2,1,0:T(8,128)S(1)}, u32[]{:S(2)}, u32[]{:S(2)}) collective-permute-start(f32[16,64,256]{2,1,0:T(8,128)S(1)} %get-tuple-element.22), channel_id=1, source_target_pairs={{0,1},{1,0},{2,3},{3,2},{4,5},{5,4},{6,7},{7,6},{8,9},{9,8},{10,11... | collective-permute-start | bytes 3145736 | tf_op jit(solution)/shard_map/ppermute | solution.py:33
  166.8 41.3 %collective-permute-start.5 = (f32[16,64,256]{2,1,0:T(8,128)S(1)}, f32[16,64,256]{2,1,0:T(8,128)S(1)}, u32[]{:S(2)}, u32[]{:S(2)}) collective-permute-start(f32[16,64,256]{2,1,0:T(8,128)S(1)} %get-tuple-element.23), channel_id=1, source_target_pairs={{0,2},{1,3},{2,0},{3,1},{4,6},{5,7},{6,4},{7,5},{8,10},{9,11},{10,... | collective-permute-start | bytes 3145736 | tf_op jit(solution)/shard_map/ppermute | solution.py:33
  167.5 42.1 %copy-start.18 = (f32[64]{0:T(128)S(1)}, f32[64]{0:T(128)}, u32[]{:S(2)}) copy-start(f32[64]{0:T(128)} %param.24) | copy-start | bytes 772
  203.0 39.3 %collective-permute-start.6 = (f32[16,64,256]{2,1,0:T(8,128)}, f32[16,64,256]{2,1,0:T(8,128)}, u32[]{:S(2)}, u32[]{:S(2)}) collective-permute-start(f32[16,64,256]{2,1,0:T(8,128)} %get-tuple-element.24), channel_id=1, source_target_pairs={{0,3},{1,2},{2,1},{3,0},{4,7},{5,6},{6,5},{7,4},{8,11},{9,10},{10,... | collective-permute-start | bytes 3145736 | tf_op jit(solution)/shard_map/ppermute | solution.py:33
  204.2 73.0 %collective-permute-start.16 = (f32[16,64,256]{2,1,0:T(8,128)}, f32[16,64,256]{2,1,0:T(8,128)S(1)}, u32[]{:S(2)}, u32[]{:S(2)}) collective-permute-start(f32[16,64,256]{2,1,0:T(8,128)} %get-tuple-element.26), channel_id=1, source_target_pairs={{4,0},{5,1},{6,2},{7,3},{8,4},{9,5},{10,6},{11,7},{12,8},{13,9},{1... | collective-permute-start | bytes 3145736 | tf_op jit(solution)/shard_map/ppermute | solution.py:33
  205.5 93.0 %collective-permute-start.17 = (f32[16,64,256]{2,1,0:T(8,128)}, f32[16,64,256]{2,1,0:T(8,128)S(1)}, u32[]{:S(2)}, u32[]{:S(2)}) collective-permute-start(f32[16,64,256]{2,1,0:T(8,128)} %get-tuple-element.27), channel_id=1, source_target_pairs={{4,1},{5,0},{6,3},{7,2},{8,5},{9,4},{10,7},{11,6},{12,9},{13,8},{1... | collective-permute-start | bytes 3145736 | tf_op jit(solution)/shard_map/ppermute | solution.py:33
  206.8 3.4 %copy-start.10 = (f32[16,64,256]{2,1,0:T(8,128)}, f32[16,64,256]{2,1,0:T(8,128)S(1)}, u32[]{:S(2)}) copy-start(f32[16,64,256]{2,1,0:T(8,128)S(1)} %collective-permute-done.4.strip) | copy-start | bytes 3145732
  206.8 91.7 %collective-permute-start.18 = (f32[16,64,256]{2,1,0:T(8,128)}, f32[16,64,256]{2,1,0:T(8,128)}, u32[]{:S(2)}, u32[]{:S(2)}) collective-permute-start(f32[16,64,256]{2,1,0:T(8,128)} %get-tuple-element.28), channel_id=1, source_target_pairs={{4,2},{5,3},{6,0},{7,1},{8,6},{9,7},{10,4},{11,5},{12,10},{13,11},... | collective-permute-start | bytes 3145736 | tf_op jit(solution)/shard_map/ppermute | solution.py:33
  208.1 1.5 copy-start.9
  208.2 90.4 %collective-permute-start.19 = (f32[16,64,256]{2,1,0:T(8,128)S(1)}, f32[16,64,256]{2,1,0:T(8,128)}, u32[]{:S(2)}, u32[]{:S(2)}) collective-permute-start(f32[16,64,256]{2,1,0:T(8,128)S(1)} %get-tuple-element.29), channel_id=1, source_target_pairs={{4,3},{5,2},{6,1},{7,0},{8,7},{9,6},{10,5},{11,4},{12,11},{13,10},... | collective-permute-start | bytes 3145736 | tf_op jit(solution)/shard_map/ppermute | solution.py:33
  235.0 3.4 %copy-start.16 = (f32[1,1024]{1,0:T(1,128)S(1)}, f32[1,1024]{1,0:T(1,128)}, u32[]{:S(2)}) copy-start(f32[1,1024]{1,0:T(1,128)} %param.19) | copy-start | bytes 12292
  277.2 21.3 %copy-start.11 = (f32[16,64,256]{2,1,0:T(8,128)}, f32[16,64,256]{2,1,0:T(8,128)S(1)}, u32[]{:S(2)}) copy-start(f32[16,64,256]{2,1,0:T(8,128)S(1)} %collective-permute-done.16.refs_0_) | copy-start | bytes 3145732
  298.6 1.0 copy-start.12

commit v2 on v1

v2 whole, which is shorter than its diff:
```python
import functools

import jax
import jax.numpy as jnp
from jax import lax
from jax.experimental import pallas as pl
from jax.experimental.pallas import tpu as pltpu
from jax.sharding import PartitionSpec as P

STEPS = 4
BIAS_TERMS = 3
BIAS_PAD = 16
PAIR = 2
GROUP = 8
LANES = 128
BLOCK = 128

exact_mode = lax.Precision.HIGHEST
MIB = 2**20
ROOM = 56 * MIB
COST = pl.CostEstimate(flops=10**6, bytes_accessed=10**5, transcendentals=0)
LONG = pl.CostEstimate(flops=10**12, bytes_accessed=10**9, transcendentals=0)


def send(value, shift, turn, swap):
    windows, count = lax.axis_size("win"), lax.axis_size("space")
    pairs = []
    for window in range(max(0, -shift), min(windows, windows - shift)):
        for index in range(count):
            other = meet(index // PAIR, turn, count // PAIR) * PAIR + (index % PAIR ^ swap)
            pairs.append((window * count + index, (window + shift) * count + other))
    if all(source == target for source, target in pairs):
        return value
    return lax.ppermute(value, ("win", "space"), pairs)


def meet(group, turn, groups):
    if groups & (groups - 1) == 0:
        return group ^ turn
    return (turn - group + groups) % groups


def ignoring(kernel, first, number):
    def run(*refs):
        kernel(*refs[:first], *refs[first + number :])

    return run


def later(value, *earlier, cost=None):
    return pl.pallas_call(
        lambda *refs: None,
        in_specs=[pl.BlockSpec(memory_space=pl.ANY)] * (1 + len(earlier)),
        out_specs=pl.BlockSpec(memory_space=pl.ANY),
        out_shape=jax.ShapeDtypeStruct(value.shape, value.dtype),
        input_output_aliases={0: 0},
        cost_estimate=COST if cost is None else cost,
        name="later",
    )(value, *earlier)


def full_spec(array):
    return pl.BlockSpec(array.shape, lambda *_: (0,) * array.ndim)


def parts_of(row):
    cols = row.shape[-1]
    return tuple(row[..., first : first + LANES] for first in range(0, cols, LANES))


def step_row(rows, weights):
    below, centre, above = rows
    width = centre[0].shape[-1]
    lane = lax.broadcasted_iota(jnp.int32, centre[0].shape, 1)
    first, last = lane == 0, lane == width - 1
    lefts = [pltpu.roll(part, 1, 1) for part in centre]
    rights = [pltpu.roll(part, width - 1, 1) for part in centre]
    results = []
    for at, part in enumerate(centre):
        keep, row_up, row_down, col_up, col_down = weights
        left = jnp.where(first, lefts[at - 1] if at else 0.0, lefts[at])
        right = jnp.where(last, rights[at + 1] if at + 1 < len(centre) else 0.0, rights[at])
        sides = col_up * right + col_down * left
        results.append((keep * part + sides) + (row_up * above[at] + row_down * below[at]))
    return tuple(results)


def all_steps(source, target, weights, rows):
    cols = source.shape[-1]
    for field in (source, target):
        for edge in (0, rows + 1):
            field[edge] = jnp.zeros(field.shape[1:], jnp.float32)
    block = min(BLOCK, rows)
    for _ in range(STEPS):

        def visit(number, carry, source=source, target=target):
            first = number * block
            for row in range(block):
                below, centre, above = (parts_of(source[first + row + at]) for at in range(3))
                for at, part in enumerate(step_row((below, centre, above), weights)):
                    target[first + row + 1, :, at * LANES : at * LANES + part.shape[-1]] = part
            return carry

        lax.fori_loop(0, rows // block, visit, 0)
        source, target = target, source
    return source


def out_kernel(count, place, weights, field, *refs):
    strips, (work, other) = refs[:count], refs[count:]
    rows = field.shape[1]

    def turn(number, carry):
        first = pl.multiple_of(number * GROUP, GROUP)
        work[pl.ds(first + 1, GROUP)] = jnp.swapaxes(field[:, pl.ds(first, GROUP), :], 0, 1)
        return carry

    lax.fori_loop(0, rows // GROUP, turn, 0, unroll=4)
    done = all_steps(work, other, [weights[term] for term in range(5)], rows)
    for number, strip in enumerate(strips):
        strip[...] = done[pl.ds(place[number] + 1, strip.shape[0])]


def weight_spec(depth):
    return pl.BlockSpec((5, depth, LANES), lambda step, *_: (0, step, 0))


def stencil_out(field, weights, starts, heights, after):
    levels, rows, cols = field.shape
    depth = min(8, levels)
    return pl.pallas_call(
        ignoring(functools.partial(out_kernel, len(heights)), 3, len(after)),
        grid_spec=pltpu.PrefetchScalarGridSpec(
            num_scalar_prefetch=1,
            grid=(levels // depth,),
            in_specs=[
                weight_spec(depth),
                pl.BlockSpec((depth, rows, cols), lambda step, *_: (step, 0, 0)),
            ]
            + [pl.BlockSpec(memory_space=pl.ANY)] * len(after),
            out_specs=[
                pl.BlockSpec((height, depth, cols), lambda step, *_: (0, step, 0))
                for height in heights
            ],
            scratch_shapes=[pltpu.VMEM((rows + 2, depth, cols), jnp.float32)] * 2,
        ),
        out_shape=[jax.ShapeDtypeStruct((height, levels, cols), jnp.float32) for height in heights],
        compiler_params=pltpu.CompilerParams(vmem_limit_bytes=ROOM),
        cost_estimate=LONG,
        name="stencil_out",
    )(starts, weights, field, *after)


def in_kernel(count, height, place, core, weights, *refs):
    strips, base, results = refs[:count], refs[count], refs[count + 1 : 2 * count + 1]
    whole, out, state_out, work, other = refs[2 * count + 1 :]
    rows = out.shape[1]
    for turn in range(count):
        work[pl.ds(place[turn] * height + 1, height)] = strips[turn][...]
    done = all_steps(work, other, [weights[term] for term in range(5)], rows)

    def finish(group, carry):
        first = pl.multiple_of(group * GROUP, GROUP)
        span = (slice(None), pl.ds(first, GROUP), slice(None))
        out[span] = base[span] - jnp.swapaxes(done[pl.ds(first + 1, GROUP)], 0, 1)
        return carry

    lax.fori_loop(0, rows // GROUP, finish, 0, unroll=4)
    for turn in range(count):
        span = pl.ds(pl.multiple_of(place[turn] * height, 8), height)
        state_out[:, span, :] = whole[:, span, :] - results[turn][...]


def finish_both(strips, base, results, whole, weights, place, core):
    levels, rows, cols = base.shape
    count = place.shape[0]
    height = rows // count
    depth = min(8, levels)
    steps = levels // depth
    far = pl.BlockSpec((height, depth, cols), lambda step, *_: (0, step, 0))
    if levels % 8:
        strips = [
            lax.dynamic_slice_in_dim(strip, core[0] * levels, levels, 1)
            if strip.shape[1] != levels
            else strip
            for strip in strips
        ]
        near = far
    else:
        near = pl.BlockSpec(
            (height, depth, cols), lambda step, place, core: (0, core[0] * steps + step, 0)
        )
    slab_spec = pl.BlockSpec((depth, rows, cols), lambda step, *_: (step, 0, 0))
    result_spec = pl.BlockSpec((depth, height, cols), lambda step, *_: (step, 0, 0))
    return pl.pallas_call(
        functools.partial(in_kernel, count, height),
        grid_spec=pltpu.PrefetchScalarGridSpec(
            num_scalar_prefetch=2,
            grid=(steps,),
            in_specs=[weight_spec(depth)]
            + [far if strip.shape[1] == levels else near for strip in strips]
            + [slab_spec]
            + [result_spec] * count
            + [slab_spec],
            out_specs=[slab_spec, slab_spec],
            scratch_shapes=[pltpu.VMEM((rows + 2, depth, cols), jnp.float32)] * 2,
        ),
        out_shape=[jax.ShapeDtypeStruct(base.shape, jnp.float32)] * 2,
        compiler_params=pltpu.CompilerParams(vmem_limit_bytes=ROOM),
        cost_estimate=COST,
        name="finish_both",
    )(place, core, weights, *strips, base, *results, whole)


def net_kernel(groups, levels, rows, cols, rows_in, at, core, *refs):
    count = groups * PAIR
    strips = refs[:count]
    path, gate, first, second = refs[count : count + 4]
    outs, (values, paths, results) = refs[count + 4 : -3], refs[-3:]
    for side in range(PAIR):

        @pl.when(core[0] == side)
        def _():
            for turn in range(count):
                start = (turn // PAIR) * PAIR * levels + (side ^ (turn % PAIR)) * levels
                strip = strips[turn][...]
                strip = strip if rows_in else jnp.swapaxes(strip, 0, 1)
                values[:, start : start + levels, :] = strip

    paths[...] = jnp.swapaxes(path[...].astype(jnp.float32), 0, 1).astype(jnp.bfloat16)
    term = lax.broadcasted_iota(jnp.int32, (BIAS_PAD, cols), 0)
    ones = jnp.where(term < BIAS_TERMS, 1.0, 0.0).astype(jnp.bfloat16)

    def visit(row, carry):
        centre = values[row]
        half = jnp.dot(
            gate[...], jnp.concatenate([paths[row], ones], 0), preferred_element_type=jnp.float32
        )
        hidden = jnp.dot(first[...], centre.astype(jnp.bfloat16), preferred_element_type=jnp.float32)
        bent = jnp.tanh(half)
        slope = (1.0 + bent) * (1.0 + half * (1.0 - bent))
        hidden = (slope * hidden).astype(jnp.bfloat16)
        results[row] = centre + jnp.dot(second[...], hidden, preferred_element_type=jnp.float32)
        return carry

    lax.fori_loop(0, rows, visit, 0, unroll=2)
    def put(out, start, depth):
        result = results[:, start : start + depth, :]
        out[...] = jnp.swapaxes(result, 0, 1) if rows_in else result

    if rows_in:
        for side in range(PAIR):

            @pl.when(core[0] == side)
            def _():
                for turn in range(count):
                    put(outs[turn], (turn // PAIR * PAIR + (side ^ (turn % PAIR))) * levels, levels)

    else:
        for group in range(groups):
            put(outs[group], group * PAIR * levels, PAIR * levels)


def network(strips, offsets, core, path, gate, first, second, after, rows_in):
    count = len(strips)
    groups = count // PAIR
    total, height, cols = path.shape
    levels = total // count
    rows = min(16, height)
    if rows_in:
        out_specs = [pl.BlockSpec((levels, rows, cols), lambda step, *_: (0, step, 0))] * count
        out_shapes = [(levels, height, cols)] * count
    else:
        depth = PAIR * levels
        out_specs = [pl.BlockSpec((rows, depth, cols), lambda step, *_: (step, 0, 0))] * groups
        out_shapes = [(height, depth, cols)] * groups
    in_specs = []
    for turn in range(count):
        if rows_in:
            spec = pl.BlockSpec(
                (rows, levels, cols), lambda step, at, core, turn=turn: (at[turn] + step, 0, 0)
            )
        else:
            spec = pl.BlockSpec(
                (levels, rows, cols), lambda step, at, core, turn=turn: (0, at[turn] + step, 0)
            )
        in_specs.append(spec)
    return pl.pallas_call(
        ignoring(functools.partial(net_kernel, groups, levels, rows, cols, rows_in), count + 6, len(after)),
        grid_spec=pltpu.PrefetchScalarGridSpec(
            num_scalar_prefetch=2,
            grid=(height // rows,),
            in_specs=in_specs
            + [pl.BlockSpec((total, rows, cols), lambda step, *_: (0, step, 0))]
            + [full_spec(gate), full_spec(first), full_spec(second)]
            + [pl.BlockSpec(memory_space=pl.ANY)] * len(after),
            out_specs=out_specs,
            scratch_shapes=[
                pltpu.VMEM((rows, total, cols), jnp.float32),
                pltpu.VMEM((rows, total, cols), jnp.bfloat16),
                pltpu.VMEM((rows, total, cols), jnp.float32),
            ],
        ),
        out_shape=[jax.ShapeDtypeStruct(shape, jnp.float32) for shape in out_shapes],
        compiler_params=pltpu.CompilerParams(vmem_limit_bytes=ROOM),
        cost_estimate=COST if rows_in else LONG,
        name="network",
    )(offsets // rows, core, *strips, path, gate, first, second, *after)


def halves(value):
    high = value.astype(jnp.bfloat16)
    return high, (value - high.astype(jnp.float32)).astype(jnp.bfloat16)


def correlate_kernel(depth, spread, row_factor, col_factor, fields, state, out, left, right):
    step = pl.program_id(0)
    same = (((1,), (1,)), ((), ()))

    @pl.when(step == 0)
    def _():
        pairs = [
            lax.dot_general(
                factor[...], factor[...], same, precision=exact_mode,
                preferred_element_type=jnp.float32,
            )
            for factor in (row_factor, col_factor)
        ]
        high, low = halves(pairs[0])
        left[...] = jnp.concatenate([high, low, high], 1)
        high, low = halves(pairs[1])
        right[...] = jnp.concatenate([high, low, high], 0)

    rows, cols = fields.shape[1:]
    high, low = halves(fields[...].reshape(depth * rows, cols))
    inner = jnp.dot(
        jnp.concatenate([high, high, low], 1), right[...], preferred_element_type=jnp.float32
    )
    high, low = halves(inner)
    for item in range(depth):
        span = slice(item * rows, (item + 1) * rows)
        outer = jnp.dot(
            left[...],
            jnp.concatenate([high[span], high[span], low[span]], 0),
            preferred_element_type=jnp.float32,
        )
        scale = spread[step * depth + item] * spread[step * depth + item]
        out[item] = scale * outer + state[item]


def correlate(fields, state, spread, row_factor, col_factor, after):
    levels, rows, cols = fields.shape
    depth = min(4, levels)
    slab_spec = pl.BlockSpec((depth, rows, cols), lambda step, *_: (step, 0, 0))
    return pl.pallas_call(
        ignoring(functools.partial(correlate_kernel, depth), 5, len(after)),
        grid_spec=pltpu.PrefetchScalarGridSpec(
            num_scalar_prefetch=1,
            grid=(levels // depth,),
            in_specs=[full_spec(row_factor), full_spec(col_factor), slab_spec, slab_spec]
            + [pl.BlockSpec(memory_space=pl.ANY)] * len(after),
            out_specs=slab_spec,
            scratch_shapes=[
                pltpu.VMEM((rows, 3 * rows), jnp.bfloat16),
                pltpu.VMEM((3 * cols, cols), jnp.bfloat16),
            ],
        ),
        out_shape=jax.ShapeDtypeStruct(fields.shape, jnp.float32),
        compiler_params=pltpu.CompilerParams(vmem_limit_bytes=ROOM),
        cost_estimate=LONG,
        name="correlate",
    )(spread, row_factor, col_factor, fields, state, *after)


def observe_kernel(group, row_index, col_index, duals, state, mult, base, seen, picked, found):
    count = picked.shape[0]
    base[...] = mult[...]
    picked[...] = jnp.zeros_like(picked)
    lane = lax.broadcasted_iota(jnp.int32, (1, state.shape[1]), 1)
    spot = lax.broadcasted_iota(jnp.int32, (8, 128), 0) * 128 + lax.broadcasted_iota(
        jnp.int32, (8, 128), 1
    )

    def collect(block, number):
        for item in range(group):
            index = block * group + item
            found[number] = index
            number = number + jnp.where(col_index[index] >= 0, 1, 0)
        return number

    number = lax.fori_loop(0, count // group - 1, collect, 0)
    for item in range(group):
        found[number + item] = count - group

    def visit(block, carry):
        for item in range(group):
            index = found[block * group + item]
            row, col = row_index[index], col_index[index]
            here = jnp.where(lane == col, state[pl.ds(row, 1), :], 0.0)
            total = here[:, 0:128]
            for first in range(128, state.shape[1], 128):
                total = total + here[:, first : first + 128]
            picked[pl.ds(index, 1), :] = total
            top = pl.multiple_of((row >> 3) << 3, 8)
            side = pl.multiple_of(jnp.maximum((col >> 7) << 7, 0), 128)
            tile = (pl.ds(top, 8), pl.ds(side, 128))
            hit = spot == jnp.where(col < 0, -1, ((row & 7) << 7) + (col & 127))
            base[tile] = base[tile] + jnp.where(hit, duals[index], 0.0)
        return carry

    lax.fori_loop(0, (number + group - 1) // group, visit, 0)
    ones = jnp.ones((8, 128), jnp.float32)
    seen[...] = lax.dot_general(
        ones, picked[...], (((1,), (1,)), ((), ())), precision=exact_mode,
        preferred_element_type=jnp.float32,
    )


def observe(row_index, col_index, duals, state, mult, after):
    count = duals.shape[0]
    row_index = jnp.pad(row_index, (0, GROUP))
    col_index = jnp.pad(col_index, (0, GROUP), constant_values=-1)
    duals = jnp.pad(duals, (0, GROUP))
    vmem = pl.BlockSpec(memory_space=pltpu.VMEM)
    smem = pl.BlockSpec(memory_space=pltpu.SMEM)
    base, seen = pl.pallas_call(
        ignoring(functools.partial(observe_kernel, GROUP), 5, len(after)),
        in_specs=[smem, smem, smem, vmem, vmem] + [pl.BlockSpec(memory_space=pl.ANY)] * len(after),
        out_specs=[vmem, vmem],
        out_shape=[
            jax.ShapeDtypeStruct(mult.shape, jnp.float32),
            jax.ShapeDtypeStruct((8, count + GROUP), jnp.float32),
        ],
        scratch_shapes=[
            pltpu.VMEM((count + GROUP, 128), jnp.float32),
            pltpu.SMEM((count + 2 * GROUP,), jnp.int32),
        ],
        compiler_params=pltpu.CompilerParams(vmem_limit_bytes=ROOM),
        cost_estimate=LONG,
        name="observe",
    )(row_index, col_index, duals, state, mult, *after)
    return base, seen[0, :count]


def bias_terms(bias):
    terms, rest = [], bias
    for _ in range(BIAS_TERMS):
        term = lax.reduce_precision(rest, 8, 7)
        terms.append(term.astype(jnp.bfloat16))
        rest = rest - term
    zero = jnp.zeros((bias.shape[0], BIAS_PAD - BIAS_TERMS), jnp.bfloat16)
    return jnp.concatenate([jnp.stack(terms, 1), zero], 1)


def body(
    increment,
    multiplier,
    obs_dual,
    obs_sites,
    obs_variance,
    trajectory,
    diffusion,
    drift_rows,
    drift_cols,
    spread,
    row_factor,
    col_factor,
    layer_in,
    bias_in,
    layer_out,
):
    state, mult, path = increment[0], multiplier[0], trajectory[0]
    levels, rows, cols = state.shape
    count = lax.axis_size("space")
    groups = count // PAIR
    here = lax.axis_index("space")
    group, core = here // PAIR, here % PAIR
    height = rows // count
    pair_rows = PAIR * height
    first_level = here * levels
    turns = range(groups)
    group_place = jnp.stack([meet(group, turn, groups) for turn in turns]).astype(jnp.int32)
    place = (group_place[:, None] * PAIR + (core ^ jnp.arange(PAIR))[None, :]).reshape(-1)
    place = place.astype(jnp.int32)
    core_ref = core.astype(jnp.int32)[None]

    def local(values):
        return lax.dynamic_slice_in_dim(values, first_level, levels)

    def weights(direction):
        mix, along, across = local(diffusion), direction * local(drift_rows), direction * local(drift_cols)
        terms = jnp.stack([1.0 - 4.0 * mix, mix - along, mix + along, mix - across, mix + across])
        return jnp.broadcast_to(terms[:, :, None], (5, levels, LANES))

    def swap(value, size, axis):
        return send(lax.dynamic_slice_in_dim(value, (1 - core) * size, size, axis), 0, 0, 1)

    all_duals = [send(obs_dual[0], 0, turn, side) for turn in turns for side in range(PAIR)]

    starts = jnp.stack([here * height, (here ^ 1) * height] + [group_place[turn] * pair_rows for turn in turns[1:]])
    stepped = stencil_out(
        state, weights(1.0), starts.astype(jnp.int32), [height] * PAIR + [pair_rows] * (groups - 1),
        all_duals[1:],
    )
    arrived = [send(stepped[0], 1, 0, 0), send(stepped[1], 1, 0, 1)]
    crossing = [
        send(lax.dynamic_slice_in_dim(mult, group_place[turn] * pair_rows, pair_rows, 1), 0, turn, 0)
        for turn in turns[1:]
    ]

    half = jnp.asarray(0.5, jnp.bfloat16)
    gate = jnp.concatenate([layer_in, bias_terms(bias_in)], 1) * half
    order = (
        group_place[:, None] * (PAIR * levels) + jnp.arange(PAIR * levels, dtype=jnp.int32)[None, :]
    ).reshape(-1)
    layer_in_own = jnp.take(layer_in, order, axis=1)
    layer_out_own = jnp.take(layer_out, order, axis=0)

    other_start = later(place, stepped[0])[1] * height
    own_swapped = send(lax.dynamic_slice_in_dim(mult, other_start, height, 1), 0, 0, 1)
    owned = obs_dual.shape[1]
    positions = obs_sites[0]
    duals = jnp.concatenate(all_duals)
    ordered = jnp.take(positions.reshape(3, count, owned), place, axis=1).reshape(3, -1)
    local_level = ordered[0] - first_level
    inside = (local_level >= 0) & (local_level < levels)
    row_index = jnp.where(inside, local_level * rows + ordered[1], 0)
    col_index = jnp.where(inside, ordered[2], -1)
    base, seen = observe(
        row_index, col_index, duals, state.reshape(-1, cols), mult.reshape(-1, cols),
        [stepped[0], own_swapped],
    )
    base = base.reshape(mult.shape)
    seen = seen.reshape(groups, PAIR, owned)
    seen = seen[:, 0] + send(seen[:, 1], 0, 0, 1)
    parts = [send(seen[turn], 0, turn, 0) for turn in turns]
    obs_out = obs_variance[0] * obs_dual[0] + sum(parts[1:], parts[0])
    partial = correlate(mult, state, local(spread), row_factor, col_factor, [base, *arrived[:PAIR]])

    crossing = [later(value, partial, base) for value in crossing]
    for turn in turns[1:]:
        arrived.append(send(later(stepped[turn + 1], *arrived[:PAIR], base), 1, turn, 0))

    zero = jnp.int32(0)
    mult_strips = [mult, own_swapped]
    offsets = [here * height, zero]
    for value in crossing:
        mult_strips += [value, swap(value, height, 1)]
        offsets += [core * height, zero]
    adjoint = network(
        mult_strips, jnp.stack(offsets).astype(jnp.int32), core_ref, path, gate,
        layer_out_own.T, layer_in_own.T * half, [partial, obs_out], False,
    )
    ready = adjoint[0]
    adjoint = [send(adjoint[0], -1, 0, 0)] + [send(adjoint[turn], 0, turn, 0) for turn in turns[1:]]
    state_strips, offsets = arrived[:PAIR], [zero, zero]
    for value in arrived[PAIR:]:
        value = later(value, ready, cost=LONG)
        state_strips += [value, swap(value, height, 0)]
        offsets += [core * height, zero]
    tangent = network(
        state_strips, jnp.stack(offsets).astype(jnp.int32), core_ref, path, gate,
        layer_in_own, layer_out_own * half, [ready], True,
    )
    done = tangent[0]
    tangent = [send(tangent[PAIR * turn + side], 0, turn, side) for turn in turns for side in range(PAIR)]
    adjoint = adjoint[:1] + [send(later(value, done, cost=LONG), -1, 0, 0) for value in adjoint[1:]]
    adjoint_strips = []
    for value in adjoint:
        value = later(value, done, cost=LONG)
        adjoint_strips += [value, swap(value, levels, 1)]
    mult_out, state_out = finish_both(
        adjoint_strips, base, tangent, partial, weights(-1.0), place, core_ref
    )
    return (state_out[None], obs_out[None], mult_out[None])


def solution(mesh):
    placed = (
        P("win", "space", None, None),
        P("win", "space", None, None),
        P("win", "space"),
        P("win", None, None),
        P("win", "space"),
        P("win", None, "space", None),
        P(),
        P(),
        P(),
        P(),
        P(),
        P(),
        P(),
        P(),
        P(),
    )
    return jax.shard_map(
        body,
        mesh=mesh,
        in_specs=placed,
        out_specs=(P("win", "space", None, None), P("win", "space"), P("win", "space", None, None)),
        check_vma=False,
    )
```

time: 320 us -> 281 us (0.88)
  Pallas kernels: 175 us -> 143 us
  waiting for transfers between devices: 90.5 us -> 76.6 us
  local copies, waits for them, and re-layouts: 18.1 us -> 25.2 us
  other arithmetic: 3.4 us -> 8.34 us
  starting transfers between devices: 30 us -> 25.5 us
    pallas_call x10 -> x13, Pallas kernels: 175 us -> 143 us  [the longest x2 74.1 us: network(): pl.pallas_call(ignoring(functools.partial(net_kernel, groups, levels, row...]
    ppermute x20, waiting for transfers between devices: 90.5 us -> 76.6 us  [send(): return lax.ppermute(value, ('win', 'space'), pairs)]
    dynamic_slice x1 -> x6, local copies, waits for them, and re-layouts: 4.02 us -> 10.8 us  [the longest x4 6.3 us: swap(): lax.dynamic_slice_in_dim(value, (1 - core) * size, size, axis)]
    unnamed x39 -> x79, local copies, waits for them, and re-layouts: 8.51 us -> 2.95 us
    ppermute x20, starting transfers between devices: 30 us -> 25.5 us  [send(): return lax.ppermute(value, ('win', 'space'), pairs)]
  transfers between devices with their start and end apart: 20 -> 20, of which waited for: 3 -> 7; matrix products, arithmetic and copies ran while one was open for 4% -> 10% of each run, Pallas kernels for 49% -> 44%
where the time goes in v2:
time: 281 us
  Pallas kernels  143 us (51%)
  waiting for transfers between devices  76.6 us (27%)
  starting transfers between devices  25.5 us (9%)
  local copies, waits for them, and re-layouts  25.2 us (9%)
  other arithmetic  8.34 us (3%)
    ppermute x20, waiting for transfers between devices, send(): return lax.ppermute(value, ('win', 'space'), pairs)  76.6 us
    pallas_call x2, Pallas kernels, network(): pl.pallas_call(ignoring(functools.partial(net_kernel, groups, levels, row...  74.1 us
    ppermute x20, starting transfers between devices, send(): return lax.ppermute(value, ('win', 'space'), pairs)  25.5 us
    pallas_call x1, Pallas kernels, observe(): pl.pallas_call(ignoring(functools.partial(observe_kernel, GROUP), 5, len(...  25 us
    pallas_call x1, Pallas kernels, finish_both(): pl.pallas_call(functools.partial(in_kernel, count, height), grid_spec=plt...  18.3 us
    pallas_call x1, Pallas kernels, stencil_out(): pl.pallas_call(ignoring(functools.partial(out_kernel, len(heights)), 3, l...  14.5 us
    pallas_call x1, Pallas kernels, correlate(): pl.pallas_call(ignoring(functools.partial(correlate_kernel, depth), 5, le...  11.1 us
    dynamic_slice x4, local copies, waits for them, and re-layouts, swap(): lax.dynamic_slice_in_dim(value, (1 - core) * size, size, axis)  6.3 us
  transfers between devices with their start and end apart: 20, of which 7 were waited for; matrix products, arithmetic and copies ran while one was open for 10% of the time, Pallas kernels for 44%

profile of v2, /device:TPU:0, one launch (start us, length us, event | category | flops | bytes accessed | tf_op | source)
XLA Modules:
  0.0 280.5 jit_solution(11522987749556920920)
XLA Ops:
  0.6 2.4 collective-permute-start.2
  3.1 0.6 collective-permute-start.1
  3.8 3.2 %dynamic-slice_bitcast_fusion = f32[16,128,256]{2,1,0:T(8,128)} fusion(f32[1,16,256,256]{3,2,1,0:T(8,128)} %param.16, s32[]{:T(128)S(6)} %select_n.109), kind=kLoop, calls=%fused_computation.3 | loop fusion | bytes 4194308 | tf_op jit(solution)/shard_map/dynamic_slice | solution.py:507
  6.9 1.7 collective-permute-start.4
  9.2 0.5 fusion.6
  9.8 0.6 subtract_bitcast_fusion
  10.4 0.6 subtract_bitcast_fusion.1
  11.1 0.6 gather_fusion
  11.8 0.7 slice_select_fusion
  12.4 0.7 pad_add_fusion.3.refs_0_
  13.1 0.5 copy.51.refs_0_
  13.6 0.7 broadcast_in_dim.68.refs_1_
  14.3 14.5 %stencil_out.1 = (f32[64,16,256]{2,1,0:T(8,128)}, f32[64,16,256]{2,1,0:T(8,128)}, f32[128,16,256]{2,1,0:T(8,128)}) custom-call(s32[3]{0:T(128)} %pad_add_fusion.3.refs_0_, f32[5,16,128]{2,1,0:T(8,128)} %broadcast_in_dim.68.refs_1_, f32[16,256,256]{2,1,0:T(8,128)} %bitcast.88, f32[1024]{0:T(1024)} %copy-done.20, f32[1024]{0:T(1024)} %copy-done.18, ...), custom_call_target="tpu_custom_call" | custom-call | flops 999999995904 | bytes 1000000000 | tf_op jit(solution)/shard_map/stencil_out/pallas_call | solution.py:131
  28.9 1.2 slice.30
  30.7 1.3 dynamic-slice_bitcast_fusion.1
  32.2 0.7 dynamic_slice.44.refs_0_
  32.9 0.6 pad.11.refs_0_
  33.5 0.6 pad.12.refs_1_
  34.3 1.4 gather_fusion.2
  35.7 0.7 gather_fusion.1
  36.4 0.2 stack.101
  36.6 0.2 stack.100
  36.8 0.2 stack.99
  37.0 0.6 concatenate.15
  37.7 0.8 broadcast_multiply_fusion.1
  38.5 0.7 broadcast_multiply_fusion.refs_7_
  39.3 4.4 %collective-permute-start.5 = (f32[64,16,256]{2,1,0:T(8,128)}, f32[64,16,256]{2,1,0:T(8,128)}, u32[]{:S(2)}, u32[]{:S(2)}) collective-permute-start(f32[64,16,256]{2,1,0:T(8,128)} %get-tuple-element.16.refs_1_.refs_5_), channel_id=1, source_target_pairs={{0,4},{1,5},{2,6},{3,7},{4,8},{5,9},{6,10},{7,11},{8,12},{9,13},{1... | collective-permute-start | bytes 3145736 | tf_op jit(solution)/shard_map/ppermute | solution.py:34
  43.7 3.2 %collective-permute-start.6 = (f32[64,16,256]{2,1,0:T(8,128)}, f32[64,16,256]{2,1,0:T(8,128)}, u32[]{:S(2)}, u32[]{:S(2)}) collective-permute-start(f32[64,16,256]{2,1,0:T(8,128)} %get-tuple-element.18), channel_id=1, source_target_pairs={{0,5},{1,4},{2,7},{3,6},{4,9},{5,8},{6,11},{7,10},{8,13},{9,12},{1... | collective-permute-start | bytes 3145736 | tf_op jit(solution)/shard_map/ppermute | solution.py:34
  46.9 0.6 select_maximum_fusion.refs_2_
  47.5 25.0 %observe.1 = (f32[4096,256]{1,0:T(8,128)}, f32[8,4104]{1,0:T(8,128)}) custom-call(s32[4104]{0:T(1024)} %pad.11.refs_0_, s32[4104]{0:T(1024)} %pad.12.refs_1_, f32[4104]{0:T(1024)} %select_maximum_fusion.refs_2_, f32[4096,256]{1,0:T(8,128)} %bitcast.89, f32[4096,256]{1,0:T(8,128)} %bitcast.70, f32[64,16,256]{2,1,0:T(8,128)} %get-tuple-element.16.refs_1_.refs_5_, ...), custom_call_target="tpu_custom_call" | custom-call | flops 999999995904 | bytes 1000000000 | tf_op jit(solution)/shard_map/observe/pallas_call | solution.py:426
  72.5 16.0 %collective-permute-done.6.refs_7_.refs_2_.refs_3_ = f32[64,16,256]{2,1,0:T(8,128)} collective-permute-done((f32[64,16,256]{2,1,0:T(8,128)}, f32[64,16,256]{2,1,0:T(8,128)}, u32[]{:S(2)}, u32[]{:S(2)}) %collective-permute-start.6) | collective-permute-done | bytes 1048608 | tf_op jit(solution)/shard_map/ppermute | solution.py:34
  88.5 11.1 %correlate.1.refs_1_.refs_10_.refs_9_ = f32[16,256,256]{2,1,0:T(8,128)} custom-call(f32[16]{0:T(128)} %dynamic_slice.44.refs_0_, f32[256,256]{1,0:T(8,128)} %refs_1_.1, f32[256,256]{1,0:T(8,128)} %refs_2_.1, f32[16,256,256]{2,1,0:T(8,128)} %bitcast.71, f32[16,256,256]{2,1,0:T(8,128)} %bitcast.90, f32[16,256,256]{2,1,0:T(8,128)} %bitcast.66, ...), custom_call_target="tpu_custom_call" | custom-call | flops 999999995904 | bytes 1000000000 | tf_op jit(solution)/shard_map/correlate/pallas_call | solution.py:355
  99.6 0.9 slice_reduce_fusion
  100.6 1.4 constant_dynamic-slice_fusion.3
  102.1 0.6 collective-permute-start.8
  102.7 0.8 multiply_bitcast_fusion
  103.5 1.3 collective-permute-done.8
  104.8 0.6 collective-permute-start.9
  105.4 0.6 and_select_fusion.1.refs_0_
  106.0 0.8 copy.42.refs_8_
  106.8 6.3 %collective-permute-start.11 = (f32[128,16,256]{2,1,0:T(8,128)}, f32[128,16,256]{2,1,0:T(8,128)}, u32[]{:S(2)}, u32[]{:S(2)}) collective-permute-start(f32[128,16,256]{2,1,0:T(8,128)} %later.9), channel_id=1, source_target_pairs={{0,6},{1,7},{2,4},{3,5},{4,10},{5,11},{6,8},{7,9},{8,14},{9,15},{1... | collective-permute-start | bytes 6291464 | tf_op jit(solution)/shard_map/ppermute | solution.py:34
  113.2 0.6 add_add_fusion.refs_11_
  113.8 1.0 copy-done.34
  114.8 37.0 %network.2 = (f32[64,32,256]{2,1,0:T(8,128)}, f32[64,32,256]{2,1,0:T(8,128)}) custom-call(s32[4]{0:T(128)} %and_select_fusion.1.refs_0_, s32[1]{0:T(128)} %bitcast.2.refs_1_.core, f32[16,256,256]{2,1,0:T(8,128)} %bitcast.72, f32[16,64,256]{2,1,0:T(8,128)} %collective-permute-done.3.refs_6_.refs_3_, f32[16,128,256]{2,1,0:T(8,128)} %later.8.refs_4_, ...), custom_call_target="tpu_custom_call" | custom-call | flops 999999995904 | bytes 1000000000 | tf_op jit(solution)/shard_map/network/pallas_call | solution.py:288
  151.7 0.5 collective-permute-start.14
  152.3 5.9 %collective-permute-done.11.refs_0_ = f32[128,16,256]{2,1,0:T(8,128)} collective-permute-done((f32[128,16,256]{2,1,0:T(8,128)}, f32[128,16,256]{2,1,0:T(8,128)}, u32[]{:S(2)}, u32[]{:S(2)}) %collective-permute-start.11) | collective-permute-done | bytes 2097184 | tf_op jit(solution)/shard_map/ppermute | solution.py:34
  158.2 1.3 constant_dynamic-slice_fusion.2
  159.6 0.8 copy.43.refs_8_
  160.4 0.7 and_select_fusion.refs_0_
  161.1 1.5 collective-permute-start.10
  162.6 1.0 copy-done.5
  163.6 37.1 %network.3 = (f32[16,64,256]{2,1,0:T(8,128)}, f32[16,64,256]{2,1,0:T(8,128)}, f32[16,64,256]{2,1,0:T(8,128)}, f32[16,64,256]{2,1,0:T(8,128)}) custom-call(s32[4]{0:T(128)} %and_select_fusion.refs_0_, s32[1]{0:T(128)} %bitcast.2.refs_1_.core, f32[64,16,256]{2,1,0:T(8,128)} %collective-permute-done.5.refs_6_.refs_1_.refs_2_, ...), custom_call_target="tpu_custom_call" | custom-call | flops 1000000 | bytes 100000 | tf_op jit(solution)/shard_map/network/pallas_call | solution.py:288
  200.6 0.5 collective-permute-start.17
  201.1 0.5 collective-permute-start.18
  201.7 0.9 collective-permute-start.19
  202.6 0.5 collective-permute-done.14.refs_0_
  203.1 1.3 collective-permute-start.15
  204.4 7.9 %collective-permute-done.10.refs_0_ = f32[64,32,256]{2,1,0:T(8,128)} collective-permute-done((f32[64,32,256]{2,1,0:T(8,128)}, f32[64,32,256]{2,1,0:T(8,128)}, u32[]{:S(2)}, u32[]{:S(2)}) %collective-permute-start.10) | collective-permute-done | bytes 2097184 | tf_op jit(solution)/shard_map/ppermute | solution.py:34
  212.3 2.3 constant_dynamic-slice_fusion.1
  214.5 42.5 %collective-permute-done.15.refs_0_ = f32[64,32,256]{2,1,0:T(8,128)} collective-permute-done((f32[64,32,256]{2,1,0:T(8,128)}, f32[64,32,256]{2,1,0:T(8,128)}, u32[]{:S(2)}, u32[]{:S(2)}) %collective-permute-start.15) | collective-permute-done | bytes 2097184 | tf_op jit(solution)/shard_map/ppermute | solution.py:34
  257.0 1.3 constant_dynamic-slice_fusion
  258.5 2.5 collective-permute-done.16.refs_3_
  261.1 0.8 broadcast_in_dim.67.weights
  262.0 18.3 %finish_both.1 = (f32[16,256,256]{2,1,0:T(8,128)}, f32[16,256,256]{2,1,0:T(8,128)}) custom-call(s32[4]{0:T(128)} %copy-done.29, s32[1]{0:T(128)} %bitcast.2.refs_1_.core, f32[5,16,128]{2,1,0:T(8,128)} %broadcast_in_dim.67.weights, f32[64,32,256]{2,1,0:T(8,128)} %later.11.refs_0_, f32[64,16,256]{2,1,0:T(8,128)} %collective-permute-done.13.refs_1_, ...), custom_call_target="tpu_custom_call" | custom-call | flops 1000000 | bytes 100000 | tf_op jit(solution)/shard_map/finish_both/pallas_call | solution.py:195
  (127 shorter events, 1.9 us)
Async XLA Ops:
  0.6 35.0 %copy-start = (bf16[64,1024]{1,0:T(8,128)(2,1)S(1)}, bf16[64,1024]{1,0:T(8,128)(2,1)}, u32[]{:S(2)}) copy-start(bf16[64,1024]{1,0:T(8,128)(2,1)} %param.29) | copy-start | bytes 393220
  0.6 12.9 %collective-permute-start.2 = (f32[1024]{0:T(1024)}, f32[1024]{0:T(1024)S(1)}, u32[]{:S(2)}, u32[]{:S(2)}) collective-permute-start(f32[1024]{0:T(1024)} %bitcast.78), channel_id=1, source_target_pairs={{0,3},{1,2},{2,1},{3,0},{4,7},{5,6},{6,5},{7,4},{8,11},{9,10},{10,... | collective-permute-start | bytes 12296 | tf_op jit(solution)/shard_map/ppermute | solution.py:34
  3.1 10.5 %collective-permute-start.1 = (f32[1024]{0:T(1024)}, f32[1024]{0:T(1024)S(1)}, u32[]{:S(2)}, u32[]{:S(2)}) collective-permute-start(f32[1024]{0:T(1024)} %bitcast.79), channel_id=1, source_target_pairs={{0,2},{1,3},{2,0},{3,1},{4,6},{5,7},{6,4},{7,5},{8,10},{9,11},{10,... | collective-permute-start | bytes 12296 | tf_op jit(solution)/shard_map/ppermute | solution.py:34
  3.7 9.9 %collective-permute-start = (f32[1024]{0:T(1024)}, f32[1024]{0:T(1024)S(1)}, u32[]{:S(2)}, u32[]{:S(2)}) collective-permute-start(f32[1024]{0:T(1024)} %bitcast.80), channel_id=1, source_target_pairs={{0,1},{1,0},{2,3},{3,2},{4,5},{5,4},{6,7},{7,6},{8,9},{9,8},{10,11... | collective-permute-start | bytes 12296 | tf_op jit(solution)/shard_map/ppermute | solution.py:34
  3.8 5.9 %copy-start.32 = (f32[64]{0:T(128)S(1)}, f32[64]{0:T(128)}, u32[]{:S(2)}) copy-start(f32[64]{0:T(128)} %param.23) | copy-start | bytes 772
  3.8 5.9 %copy-start.33 = (f32[64]{0:T(128)S(1)}, f32[64]{0:T(128)}, u32[]{:S(2)}) copy-start(f32[64]{0:T(128)} %param.21) | copy-start | bytes 772
  3.8 6.0 %copy-start.30 = (f32[64]{0:T(128)S(1)}, f32[64]{0:T(128)}, u32[]{:S(2)}) copy-start(f32[64]{0:T(128)} %param.22) | copy-start | bytes 772
  3.8 7.2 %copy-start.10 = (s32[1,3,4096]{2,0,1:T(1,128)S(1)}, s32[1,3,4096]{2,0,1:T(1,128)}, u32[]{:S(2)}) copy-start(s32[1,3,4096]{2,0,1:T(1,128)} %param.18) | copy-start | bytes 147460
  6.9 93.6 %collective-permute-start.4 = (f32[16,128,256]{2,1,0:T(8,128)}, f32[16,128,256]{2,1,0:T(8,128)}, u32[]{:S(2)}, u32[]{:S(2)}) collective-permute-start(f32[16,128,256]{2,1,0:T(8,128)} %dynamic-slice_bitcast_fusion), channel_id=1, source_target_pairs={{0,2},{1,3},{2,0},{3,1},{4,6},{5,7},{6,4},{7,5},{8,10},{9,11},{10,... | collective-permute-start | bytes 6291464 | tf_op jit(solution)/shard_map/ppermute | solution.py:34
  8.9 19.9 %copy-start.29 = (s32[4]{0:T(128)}, s32[4]{0:T(128)S(1)}, u32[]{:S(2)}) copy-start(s32[4]{0:T(128)S(1)} %add.163.place) | copy-start | bytes 52
  9.1 0.7 copy-start.36
  10.3 18.5 %copy-start.13 = (f32[1,16]{1,0:T(1,128)}, f32[1,16]{1,0:T(1,128)S(1)}, u32[]{:S(2)}) copy-start(f32[1,16]{1,0:T(1,128)S(1)} %get-tuple-element.55) | copy-start | bytes 196
  13.6 0.7 copy-start.16
  13.6 0.7 copy-start.18
  13.6 0.7 copy-start.20
  28.8 3.3 %copy-start.31 = (s32[64]{0:T(128)S(1)}, s32[64]{0:T(128)}, u32[]{:S(2)}) copy-start(s32[64]{0:T(128)} %fusion.6) | copy-start | bytes 772
  28.8 3.3 %copy-start.37 = (s32[2,32]{1,0:T(2,128)S(1)}, s32[2,32]{1,0:T(2,128)}, u32[]{:S(2)}) copy-start(s32[2,32]{1,0:T(2,128)} %copy-done.36) | copy-start | bytes 772
  28.9 3.4 %copy-start.35 = (f32[64]{0:T(128)S(1)}, f32[64]{0:T(128)}, u32[]{:S(2)}) copy-start(f32[64]{0:T(128)} %param.24) | copy-start | bytes 772
  28.9 4.0 %copy-start.9 = (s32[1,4,1024]{2,0,1:T(1,128)S(1)}, s32[1,4,1024]{2,0,1:T(1,128)}, u32[]{:S(2)}) copy-start(s32[1,4,1024]{2,0,1:T(1,128)} %get-tuple-element.39) | copy-start | bytes 49156
  28.9 4.6 %copy-start.8 = (s32[1,4,1024]{2,0,1:T(1,128)S(1)}, s32[1,4,1024]{2,0,1:T(1,128)}, u32[]{:S(2)}) copy-start(s32[1,4,1024]{2,0,1:T(1,128)} %get-tuple-element.38) | copy-start | bytes 49156
  28.9 5.2 %copy-start.2 = (bf16[1024,64]{0,1:T(8,128)(2,1)S(1)}, bf16[1024,64]{0,1:T(8,128)(2,1)}, u32[]{:S(2)}) copy-start(bf16[1024,64]{0,1:T(8,128)(2,1)} %param.27) | copy-start | bytes 393220
  32.0 4.4 %copy-start.22 = (f32[1024]{0:T(1024)S(1)}, f32[1024]{0:T(1024)}, u32[]{:S(2)}) copy-start(f32[1024]{0:T(1024)} %param.28) | copy-start | bytes 12292
  32.0 15.5 %collective-permute-start.3 = (f32[16,64,256]{2,1,0:T(8,128)S(1)}, f32[16,64,256]{2,1,0:T(8,128)}, u32[]{:S(2)}, u32[]{:S(2)}) collective-permute-start(f32[16,64,256]{2,1,0:T(8,128)S(1)} %dynamic-slice_bitcast_fusion.1), channel_id=1, source_target_pairs={{0,1},{1,0},{2,3},{3,2},{4,5},{5,4},{6,7},{7,6},{8,9},{9,8},{10,11... | collective-permute-start | bytes 3145736 | tf_op jit(solution)/shard_map/ppermute | solution.py:34
  35.6 11.3 %copy-start.11 = (f32[1,1024]{1,0:T(1,128)S(1)}, f32[1,1024]{1,0:T(1,128)}, u32[]{:S(2)}) copy-start(f32[1,1024]{1,0:T(1,128)} %param.17) | copy-start | bytes 12292
  35.6 11.3 %copy-start.17 = (f32[1024]{0:T(1024)S(1)}, f32[1024]{0:T(1024)}, u32[]{:S(2)}) copy-start(f32[1024]{0:T(1024)} %copy-done.16) | copy-start | bytes 12292
  35.6 11.3 %copy-start.19 = (f32[1024]{0:T(1024)S(1)}, f32[1024]{0:T(1024)}, u32[]{:S(2)}) copy-start(f32[1024]{0:T(1024)} %copy-done.18) | copy-start | bytes 12292
  35.6 11.3 %copy-start.21 = (f32[1024]{0:T(1024)S(1)}, f32[1024]{0:T(1024)}, u32[]{:S(2)}) copy-start(f32[1024]{0:T(1024)} %copy-done.20) | copy-start | bytes 12292
  37.7 34.8 %copy-start.23 = (pred[64]{0:T(512)(128)(4,1)}, pred[64]{0:T(512)(128)(4,1)S(1)}, u32[]{:S(2)}) copy-start(pred[64]{0:T(512)(128)(4,1)S(1)} %compare_and_fusion.1) | copy-start | bytes 196
  39.3 49.3 %collective-permute-start.5 = (f32[64,16,256]{2,1,0:T(8,128)}, f32[64,16,256]{2,1,0:T(8,128)}, u32[]{:S(2)}, u32[]{:S(2)}) collective-permute-start(f32[64,16,256]{2,1,0:T(8,128)} %get-tuple-element.16.refs_1_.refs_5_), channel_id=1, source_target_pairs={{0,4},{1,5},{2,6},{3,7},{4,8},{5,9},{6,10},{7,11},{8,12},{9,13},{1... | collective-permute-start | bytes 3145736 | tf_op jit(solution)/shard_map/ppermute | solution.py:34
  43.7 44.8 %collective-permute-start.6 = (f32[64,16,256]{2,1,0:T(8,128)}, f32[64,16,256]{2,1,0:T(8,128)}, u32[]{:S(2)}, u32[]{:S(2)}) collective-permute-start(f32[64,16,256]{2,1,0:T(8,128)} %get-tuple-element.18), channel_id=1, source_target_pairs={{0,5},{1,4},{2,7},{3,6},{4,9},{5,8},{6,11},{7,10},{8,13},{9,12},{1... | collective-permute-start | bytes 3145736 | tf_op jit(solution)/shard_map/ppermute | solution.py:34
  100.6 2.1 copy-start.3
  100.6 2.1 copy-start.24
  100.6 5.4 %copy-start.6 = (bf16[1024,64]{0,1:T(8,128)(2,1)S(1)}, bf16[1024,64]{0,1:T(8,128)(2,1)}, u32[]{:S(2)}) copy-start(bf16[1024,64]{0,1:T(8,128)(2,1)} %get-tuple-element.37) | copy-start | bytes 393220
  102.0 11.7 %collective-permute-start.7 = (f32[16,64,256]{2,1,0:T(8,128)S(1)}, f32[16,64,256]{2,1,0:T(8,128)S(1)}, u32[]{:S(2)}, u32[]{:S(2)}) collective-permute-start(f32[16,64,256]{2,1,0:T(8,128)S(1)} %constant_dynamic-slice_fusion.3), channel_id=1, source_target_pairs={{0,1},{1,0},{2,3},{3,2},{4,5},{5,4},{6,7},{7,6},{8,9},{9,8},{10,11... | collective-permute-start | bytes 3145736 | tf_op jit(solution)/shard_map/ppermute | solution.py:34
  102.1 2.6 collective-permute-start.8
  104.8 8.4 %collective-permute-start.9 = (f32[1024]{0:T(1024)S(1)}, f32[1024]{0:T(1024)S(1)}, u32[]{:S(2)}, u32[]{:S(2)}) collective-permute-start(f32[1024]{0:T(1024)S(1)} %bitcast.87), channel_id=1, source_target_pairs={{0,2},{1,3},{2,0},{3,1},{4,6},{5,7},{6,4},{7,5},{8,10},{9,11},{10,... | collective-permute-start | bytes 12296 | tf_op jit(solution)/shard_map/ppermute | solution.py:34
  106.8 6.3 %copy-start.12 = (f32[1,1024]{1,0:T(1,128)S(1)}, f32[1,1024]{1,0:T(1,128)}, u32[]{:S(2)}) copy-start(f32[1,1024]{1,0:T(1,128)} %param.17) | copy-start | bytes 12292
  106.8 6.3 %copy-start.15 = (f32[1,1024]{1,0:T(1,128)S(1)}, f32[1,1024]{1,0:T(1,128)}, u32[]{:S(2)}) copy-start(f32[1,1024]{1,0:T(1,128)} %param.19) | copy-start | bytes 12292
  106.8 51.3 %collective-permute-start.11 = (f32[128,16,256]{2,1,0:T(8,128)}, f32[128,16,256]{2,1,0:T(8,128)}, u32[]{:S(2)}, u32[]{:S(2)}) collective-permute-start(f32[128,16,256]{2,1,0:T(8,128)} %later.9), channel_id=1, source_target_pairs={{0,6},{1,7},{2,4},{3,5},{4,10},{5,11},{6,8},{7,9},{8,14},{9,15},{1... | collective-permute-start | bytes 6291464 | tf_op jit(solution)/shard_map/ppermute | solution.py:34
  113.8 1.0 copy-start.34
  151.7 51.4 %collective-permute-start.14 = (f32[64,32,256]{2,1,0:T(8,128)}, f32[64,32,256]{2,1,0:T(8,128)}, u32[]{:S(2)}, u32[]{:S(2)}) collective-permute-start(f32[64,32,256]{2,1,0:T(8,128)} %get-tuple-element.23), channel_id=1, source_target_pairs={{0,2},{1,3},{2,0},{3,1},{4,6},{5,7},{6,4},{7,5},{8,10},{9,11},{10,... | collective-permute-start | bytes 6291464 | tf_op jit(solution)/shard_map/ppermute | solution.py:34
  158.2 1.4 copy-start.7
  159.5 3.1 %collective-permute-start.12 = (f32[64,16,256]{2,1,0:T(8,128)S(1)}, f32[64,16,256]{2,1,0:T(8,128)S(1)}, u32[]{:S(2)}, u32[]{:S(2)}) collective-permute-start(f32[64,16,256]{2,1,0:T(8,128)S(1)} %constant_dynamic-slice_fusion.2), channel_id=1, source_target_pairs={{0,1},{1,0},{2,3},{3,2},{4,5},{5,4},{6,7},{7,6},{8,9},{9,8},{10,11... | collective-permute-start | bytes 3145736 | tf_op jit(solution)/shard_map/ppermute | solution.py:34
  161.1 51.1 %collective-permute-start.10 = (f32[64,32,256]{2,1,0:T(8,128)}, f32[64,32,256]{2,1,0:T(8,128)}, u32[]{:S(2)}, u32[]{:S(2)}) collective-permute-start(f32[64,32,256]{2,1,0:T(8,128)} %get-tuple-element.20.refs_1_.refs_10_), channel_id=1, source_target_pairs={{4,0},{5,1},{6,2},{7,3},{8,4},{9,5},{10,6},{11,7},{12,8},{13,9},{1... | collective-permute-start | bytes 6291464 | tf_op jit(solution)/shard_map/ppermute | solution.py:34
  162.6 1.0 copy-start.5
  200.6 57.8 %collective-permute-start.17 = (f32[16,64,256]{2,1,0:T(8,128)}, f32[16,64,256]{2,1,0:T(8,128)}, u32[]{:S(2)}, u32[]{:S(2)}) collective-permute-start(f32[16,64,256]{2,1,0:T(8,128)} %get-tuple-element.24), channel_id=1, source_target_pairs={{0,1},{1,0},{2,3},{3,2},{4,5},{5,4},{6,7},{7,6},{8,9},{9,8},{10,11... | collective-permute-start | bytes 3145736 | tf_op jit(solution)/shard_map/ppermute | solution.py:34
  201.1 57.4 %collective-permute-start.18 = (f32[16,64,256]{2,1,0:T(8,128)}, f32[16,64,256]{2,1,0:T(8,128)}, u32[]{:S(2)}, u32[]{:S(2)}) collective-permute-start(f32[16,64,256]{2,1,0:T(8,128)} %get-tuple-element.25), channel_id=1, source_target_pairs={{0,2},{1,3},{2,0},{3,1},{4,6},{5,7},{6,4},{7,5},{8,10},{9,11},{10,... | collective-permute-start | bytes 3145736 | tf_op jit(solution)/shard_map/ppermute | solution.py:34
  201.7 56.8 %collective-permute-start.19 = (f32[16,64,256]{2,1,0:T(8,128)}, f32[16,64,256]{2,1,0:T(8,128)}, u32[]{:S(2)}, u32[]{:S(2)}) collective-permute-start(f32[16,64,256]{2,1,0:T(8,128)} %get-tuple-element.26), channel_id=1, source_target_pairs={{0,3},{1,2},{2,1},{3,0},{4,7},{5,6},{6,5},{7,4},{8,11},{9,10},{10,... | collective-permute-start | bytes 3145736 | tf_op jit(solution)/shard_map/ppermute | solution.py:34
  203.1 53.9 %collective-permute-start.15 = (f32[64,32,256]{2,1,0:T(8,128)}, f32[64,32,256]{2,1,0:T(8,128)}, u32[]{:S(2)}, u32[]{:S(2)}) collective-permute-start(f32[64,32,256]{2,1,0:T(8,128)} %later.12), channel_id=1, source_target_pairs={{4,0},{5,1},{6,2},{7,3},{8,4},{9,5},{10,6},{11,7},{12,8},{13,9},{1... | collective-permute-start | bytes 6291464 | tf_op jit(solution)/shard_map/ppermute | solution.py:34
  214.5 44.0 %collective-permute-start.13 = (f32[64,16,256]{2,1,0:T(8,128)}, f32[64,16,256]{2,1,0:T(8,128)}, u32[]{:S(2)}, u32[]{:S(2)}) collective-permute-start(f32[64,16,256]{2,1,0:T(8,128)} %constant_dynamic-slice_fusion.1), channel_id=1, source_target_pairs={{0,1},{1,0},{2,3},{3,2},{4,5},{5,4},{6,7},{7,6},{8,9},{9,8},{10,11... | collective-permute-start | bytes 3145736 | tf_op jit(solution)/shard_map/ppermute | solution.py:34
  257.0 1.4 copy-start.14
  257.0 1.4 copy-start.25
  257.0 1.4 copy-start.26
  257.0 1.4 copy-start.27
  257.0 1.4 copy-start.28
  258.3 2.7 collective-permute-start.16
  261.1 1.0 copy-start.4
  262.0 18.3 %copy-start.1 = (bf16[64,1024]{1,0:T(8,128)(2,1)S(1)}, bf16[64,1024]{1,0:T(8,128)(2,1)}, u32[]{:S(2)}) copy-start(bf16[64,1024]{1,0:T(8,128)(2,1)} %param.29) | copy-start | bytes 393220
